TPU v7x, 128 devices: a whole 4x4x4 slice. The times are simulated.
128 devices in a mesh: tile: 128 (over y, x, z, core).
Axes of the slice: x: 4, y: 4, z: 4, core: 2. Of those that a mesh axis runs over, the one named last changes fastest.
Arguments:
- features: bfloat16 [128, 16, 16, 128], P('tile'), may hold values from -6 to 6
- cotangent: bfloat16 [128, 16, 16, 128], P('tile'), may hold values from -6 to 6
- kernel_first_layer: bfloat16 [3, 3, 128, 128], replicated, may hold values from -0.1875 to 0.1875
- kernel_second_layer: bfloat16 [3, 3, 128, 128], replicated, may hold values from -0.1875 to 0.1875
- neighbors: int32 [128, 8], replicated, may hold values from -1 to 127, as said below
- turns: int32 [128, 8], replicated, may hold values from 0 to 3, as said below
Outputs:
- output: bfloat16 [128, 16, 16, 128], P('tile')
- features_gradient: bfloat16 [128, 16, 16, 128], P('tile')
- first_kernel_gradient: float32 [3, 3, 128, 128], replicated
- second_kernel_gradient: float32 [3, 3, 128, 128], replicated
Inputs may be any that keep to these rules, and one draw needn't show every extreme that they name: `neighbors`: entry (t, d) is the tile beside tile t in direction d (0 to 7: north, north-east, east, south-east, south, south-west, west, north-west), or -1 where there is none; -1 occurs only in the four diagonal directions; the entries of one row other than -1 are distinct and differ from t. Entry (t, d) is the number of counter-clockwise quarter turns that bring the tile neighbors[t, d] into tile t's orientation; it is 0 where neighbors[t, d] is -1.
All inputs are finite; a program needn't handle non-finite values.
Results may differ from a plain program's by a relative error of at most 0.0059.
Values may be sent and summed in bfloat16 or wider, within the bound.
A program may use at most 64 MiB of HBM per device.

v0:
```python
import math

import jax
import jax.numpy as jnp
from jax import lax
from jax.sharding import PartitionSpec as P

FIRST_SPACING = 1
SECOND_SPACING = 2


gelu_scale = 0.7978845608028654
gelu_cubic = 0.044715


def for_sending(x):
    return jax.tree.map(lambda a: a.astype(jnp.bfloat16) if a.dtype == jnp.float32 else a, x)


def strip_slices(tile_side, compass, rim_width):
    head_part = slice(0, rim_width)
    tail_part = slice(tile_side - rim_width, tile_side)
    whole_span = slice(0, tile_side)
    row_pick = (
        head_part,
        head_part,
        whole_span,
        tail_part,
        tail_part,
        tail_part,
        whole_span,
        head_part,
    )[compass]
    col_pick = (
        whole_span,
        tail_part,
        tail_part,
        tail_part,
        whole_span,
        head_part,
        head_part,
        head_part,
    )[compass]
    return (row_pick, col_pick)


def strip_of(strip_block, compass, rim_width):
    row_pick, col_pick = strip_slices(strip_block.shape[-2], compass, rim_width)
    return strip_block[..., row_pick, col_pick, :]


def turned(strip_block, quarter):
    return jnp.rot90(strip_block, quarter, axes=(strip_block.ndim - 3, strip_block.ndim - 2))


def select_quarter(variants, quarter_code):
    result = variants[0]
    for quarter in range(1, 4):
        result = jnp.where(quarter_code == quarter, variants[quarter], result)
    return result


def assemble(center, regions):
    top_band = jnp.concatenate([regions[7], regions[0], regions[1]], axis=-2)
    middle = jnp.concatenate([regions[6], center, regions[2]], axis=-2)
    bottom = jnp.concatenate([regions[5], regions[4], regions[3]], axis=-2)
    return jnp.concatenate([top_band, middle, bottom], axis=-3)


def padded_regions(padded, rim_width):
    tile_side = padded.shape[0] - 2 * rim_width
    near_part = slice(0, rim_width)
    mid_part = slice(rim_width, rim_width + tile_side)
    far_part = slice(rim_width + tile_side, tile_side + 2 * rim_width)
    row_parts = (near_part, near_part, mid_part, far_part, far_part, far_part, mid_part, near_part)
    col_parts = (mid_part, far_part, far_part, far_part, mid_part, near_part, near_part, near_part)
    return (
        [padded[row_parts[compass], col_parts[compass]] for compass in range(8)],
        padded[mid_part, mid_part],
    )


def to_slot(strip_piece, compass, tile_side):
    if compass in (0, 4):
        return strip_piece
    if compass in (2, 6):
        return jnp.swapaxes(strip_piece, 0, 1)
    rim_width = strip_piece.shape[0]
    return jnp.pad(strip_piece, ((0, 0), (0, tile_side - rim_width), (0, 0)))


def from_slot(slot_block, compass):
    if compass in (0, 4):
        return slot_block
    if compass in (2, 6):
        return jnp.swapaxes(slot_block, 0, 1)
    return slot_block[:, : slot_block.shape[0]]


def departing_positions(center, rim_width, neighbor_heading, neighbor_rotation, connected_tiles):
    tile_side = center.shape[0]
    candidates = []
    for direction in range(8):
        for quarter in range(4):
            strip_piece = turned(
                strip_of(center, (direction + 4 + 2 * quarter) % 8, rim_width), quarter
            )
            candidates.append(to_slot(strip_piece, direction, tile_side))
    stacked = jnp.stack(candidates)
    slot_codes = neighbor_heading * 4 + neighbor_rotation
    chooser = (
        (slot_codes[:, None] == jnp.arange(32, dtype=jnp.int32)[None, :]) & connected_tiles[:, None]
    ).astype(center.dtype)
    outgoing = jnp.dot(chooser, stacked.reshape(32, -1), preferred_element_type=jnp.float32).astype(
        center.dtype
    )
    return outgoing.reshape((chooser.shape[0],) + stacked.shape[1:])


def incoming_halo(center, received, self_row_entry):
    regions = []
    for direction in range(8):
        source = self_row_entry[direction]
        slot_block = lax.dynamic_index_in_dim(received, jnp.maximum(source, 0), 0, keepdims=False)
        region = from_slot(slot_block, direction)
        regions.append(jnp.where(source >= 0, region, jnp.zeros_like(region)))
    return assemble(center, regions)


def returned_slots(grad_padded, rim_width, self_row_entry, self_rotations, number_of_tiles):
    tile_side = grad_padded.shape[0] - 2 * rim_width
    region_list, middle_part = padded_regions(grad_padded, rim_width)
    slot_list = []
    for direction in range(8):
        variants = []
        for quarter in range(4):
            compass = (direction + 4 + 2 * quarter) % 8
            variants.append(
                to_slot(turned(region_list[direction], (4 - quarter) % 4), compass, tile_side)
            )
        slot_list.append(select_quarter(variants, self_rotations[direction]))
    stacked = jnp.stack(slot_list)
    targets = jnp.arange(number_of_tiles, dtype=jnp.int32)
    chooser = (self_row_entry[None, :] == targets[:, None]).astype(stacked.dtype)
    outgoing = jnp.dot(chooser, stacked.reshape(8, -1), preferred_element_type=jnp.float32).astype(
        stacked.dtype
    )
    return (outgoing.reshape((number_of_tiles,) + stacked.shape[1:]), middle_part)


def absorb_returns(
    middle_part, received, connected_tiles, neighbor_heading, neighbor_rotation, rim_width
):
    tile_side = middle_part.shape[0]
    compass_ids = jnp.arange(8, dtype=jnp.int32)
    side_codes = (neighbor_heading + 4 + 2 * neighbor_rotation) % 8
    chooser = ((side_codes[None, :] == compass_ids[:, None]) & connected_tiles[None, :]).astype(
        received.dtype
    )
    strip_sums = jnp.dot(
        chooser, received.reshape(received.shape[0], -1), preferred_element_type=jnp.float32
    )
    strip_sums = strip_sums.reshape((8,) + received.shape[1:])
    accumulated = middle_part.astype(jnp.float32)
    for compass in range(8):
        row_pick, col_pick = strip_slices(tile_side, compass, rim_width)
        accumulated = accumulated.at[row_pick, col_pick].add(
            from_slot(strip_sums[compass], compass)
        )
    return accumulated


def gelu_pair(preactivation):
    tanh_arg = gelu_scale * (
        preactivation + gelu_cubic * preactivation * preactivation * preactivation
    )
    tangent = jnp.tanh(tanh_arg)
    activated = 0.5 * preactivation * (1.0 + tangent)
    derivative = 0.5 * (1.0 + tangent) + 0.5 * preactivation * (
        1.0 - tangent * tangent
    ) * gelu_scale * (1.0 + 3.0 * gelu_cubic * preactivation * preactivation)
    return (activated, derivative)


def apply_convolution(padded, kernel, dilation):
    return lax.conv_general_dilated(
        padded[None],
        kernel,
        (1, 1),
        "VALID",
        rhs_dilation=(dilation, dilation),
        dimension_numbers=("NHWC", "HWIO", "NHWC"),
        preferred_element_type=jnp.float32,
    )[0]


def convolution_backward(cotangent, kernel, dilation):
    margin = 2 * dilation
    padded = jnp.pad(cotangent, ((margin, margin), (margin, margin), (0, 0)))
    flipped = jnp.swapaxes(kernel[::-1, ::-1], 2, 3)
    return apply_convolution(padded, flipped, dilation)


def kernel_gradient_fn(padded, cotangent, dilation):
    tile_side = cotangent.shape[0]
    channels = cotangent.shape[-1]
    flat_cot = cotangent.reshape(tile_side * tile_side, channels)
    rows_out = []
    for tap_row in range(3):
        tap_list = []
        for tap_col in range(3):
            window = padded[
                tap_row * dilation : tap_row * dilation + tile_side,
                tap_col * dilation : tap_col * dilation + tile_side,
            ]
            window = window.reshape(tile_side * tile_side, channels)
            tap_list.append(
                lax.dot_general(
                    window, flat_cot, (((0,), (0,)), ((), ())), preferred_element_type=jnp.float32
                )
            )
        rows_out.append(jnp.stack(tap_list))
    return jnp.stack(rows_out)


def local(features, cotangent, kernel_first_layer, kernel_second_layer, neighbors, turns):
    own_index = lax.axis_index("tile")
    number_of_tiles = lax.axis_size("tile")
    central_input = features[0]
    central_cotangent = cotangent[0]
    tile_side = central_input.shape[0]
    self_row_entry = lax.dynamic_index_in_dim(neighbors, own_index, 0, keepdims=False)
    self_rotations = lax.dynamic_index_in_dim(turns, own_index, 0, keepdims=False)
    facing_me = neighbors == own_index
    compass_ids = jnp.arange(8, dtype=jnp.int32)
    connected_tiles = jnp.any(facing_me, axis=1)
    neighbor_heading = jnp.sum(jnp.where(facing_me, compass_ids[None, :], 0), axis=1)
    neighbor_rotation = jnp.sum(jnp.where(facing_me, turns, 0), axis=1)
    dispatched_input = departing_positions(
        central_input, FIRST_SPACING, neighbor_heading, neighbor_rotation, connected_tiles
    )
    received_in = lax.all_to_all(dispatched_input, "tile", split_axis=0, concat_axis=0, tiled=True)
    bordered_input = incoming_halo(central_input, received_in, self_row_entry)
    preactivation = apply_convolution(bordered_input, kernel_first_layer, FIRST_SPACING)
    activated, derivative = gelu_pair(preactivation)
    hidden_state = activated.astype(jnp.bfloat16)
    dispatched_hidden = departing_positions(
        hidden_state, SECOND_SPACING, neighbor_heading, neighbor_rotation, connected_tiles
    )
    received_hidden = lax.all_to_all(
        dispatched_hidden, "tile", split_axis=0, concat_axis=0, tiled=True
    )
    bordered_hidden = incoming_halo(hidden_state, received_hidden, self_row_entry)
    output = apply_convolution(bordered_hidden, kernel_second_layer, SECOND_SPACING).astype(
        jnp.bfloat16
    )
    second_gradient_tilewise = kernel_gradient_fn(
        bordered_hidden, central_cotangent, SECOND_SPACING
    )
    bordered_hidden_gradient = convolution_backward(
        central_cotangent, kernel_second_layer, SECOND_SPACING
    ).astype(jnp.bfloat16)
    sent_back_hidden, central_hidden = returned_slots(
        bordered_hidden_gradient, SECOND_SPACING, self_row_entry, self_rotations, number_of_tiles
    )
    hidden_backward = lax.all_to_all(
        for_sending(sent_back_hidden), "tile", split_axis=0, concat_axis=0, tiled=True
    ).astype(sent_back_hidden.dtype)
    hidden_gradient = absorb_returns(
        central_hidden,
        hidden_backward,
        connected_tiles,
        neighbor_heading,
        neighbor_rotation,
        SECOND_SPACING,
    )
    preactivation_gradient = (hidden_gradient * derivative).astype(jnp.bfloat16)
    first_gradient_tilewise = kernel_gradient_fn(
        bordered_input, preactivation_gradient, FIRST_SPACING
    )
    bordered_input_gradient = convolution_backward(
        preactivation_gradient, kernel_first_layer, FIRST_SPACING
    ).astype(jnp.bfloat16)
    sent_back_input, inner_input = returned_slots(
        bordered_input_gradient, FIRST_SPACING, self_row_entry, self_rotations, number_of_tiles
    )
    input_backward = lax.all_to_all(
        for_sending(sent_back_input), "tile", split_axis=0, concat_axis=0, tiled=True
    ).astype(sent_back_input.dtype)
    features_gradient = absorb_returns(
        inner_input,
        input_backward,
        connected_tiles,
        neighbor_heading,
        neighbor_rotation,
        FIRST_SPACING,
    ).astype(jnp.bfloat16)
    grad_first, grad_second = lax.psum((first_gradient_tilewise, second_gradient_tilewise), "tile")
    gradient_factor = 1.0 / math.sqrt(number_of_tiles * tile_side * tile_side)
    return (
        output[None],
        features_gradient[None],
        grad_first * gradient_factor,
        grad_second * gradient_factor,
    )


def solution(mesh):
    placed = (P("tile", None, None, None), P("tile", None, None, None), P(), P(), P(), P())
    return jax.shard_map(
        local,
        mesh=mesh,
        in_specs=placed,
        out_specs=(P("tile", None, None, None), P("tile", None, None, None), P(), P()),
        check_vma=False,
    )
```

profile of v0, /device:TPU:1, one launch (start us, length us, event | category | flops | bytes accessed | tf_op | source)
XLA Modules:
  0.0 296.2 jit_solution(14787924243495533120)
XLA Ops:
  7.2 0.8 slice_bitcast_fusion.6
  7.9 0.8 fusion.121
  8.7 0.7 fusion.122
  9.7 0.7 fusion.110
  10.4 0.7 select_reduce_fusion.1
  11.2 0.4 stack.318
  11.6 0.3 fusion.3
  12.0 0.9 copy.321
  12.9 11.5 %all-to-all-start = ((bf16[128,1,16,128]{3,2,1,0:T(8,128)(2,1)}), bf16[128,1,16,128]{3,2,1,0:T(8,128)(2,1)S(1)}, u32[]{:S(2)}, u32[]{:S(2)}) async-start(bf16[128,1,16,128]{3,2,1,0:T(8,128)(2,1)} %bitcast.8), calls=%async_computation | async-start | bytes 1048576 | tf_op jit(solution)/shard_map/all_to_all | solution.py:242
  24.5 1.0 convolution_convert_fusion.4
  25.8 0.6 fusion.123
  42.0 0.6 fusion.124
  53.3 0.2 stack.360
  53.5 0.4 fusion.1
  53.9 1.2 copy.322
  55.1 0.6 fusion.130
  55.7 0.7 fusion.129
  56.4 0.7 and_reduce_fusion
  57.2 9.8 %all-to-all-start.2 = ((bf16[128,2,16,128]{3,2,1,0:T(8,128)(2,1)}), bf16[128,2,16,128]{3,2,1,0:T(8,128)(2,1)S(1)}, u32[]{:S(2)}, u32[]{:S(2)}) async-start(bf16[128,2,16,128]{3,2,1,0:T(8,128)(2,1)} %bitcast.231), calls=%async_computation.2 | async-start | bytes 2097152 | tf_op jit(solution)/shard_map/all_to_all | solution.py:266
  67.3 0.3 copy-done.10
  67.6 0.4 fusion.25
  68.2 0.2 convolution_bitcast_fusion.4
  68.4 17.7 %all-to-all-done.2 = bf16[128,2,16,128]{3,2,1,0:T(8,128)(2,1)S(1)} async-done(((bf16[128,2,16,128]{3,2,1,0:T(8,128)(2,1)}), bf16[128,2,16,128]{3,2,1,0:T(8,128)(2,1)S(1)}, u32[]{:S(2)}, u32[]{:S(2)}) %all-to-all-start.2) | async-done | bytes 1048608 | tf_op jit(solution)/shard_map/all_to_all | solution.py:266
  86.1 0.4 fusion.5
  86.6 2.0 add_select_fusion
  88.6 1.4 scatter-add.55
  90.9 0.4 fusion.4
  91.6 0.2 convolution_bitcast_fusion.9
  91.8 0.2 convolution_bitcast_fusion.10
  92.0 0.2 convolution_bitcast_fusion.11
  92.2 0.2 convolution_bitcast_fusion.12
  92.5 0.2 convolution_bitcast_fusion.14
  92.7 0.2 convolution_bitcast_fusion.15
  92.9 0.2 convolution_bitcast_fusion.16
  93.1 0.2 convolution_bitcast_fusion.17
  94.2 0.8 stack.351
  95.0 0.5 fusion
  95.9 0.3 fusion.2
  96.2 0.9 copy.333
  97.1 4.6 %all-to-all-start.3 = ((bf16[128,1,16,128]{3,2,1,0:T(8,128)(2,1)}), bf16[128,1,16,128]{3,2,1,0:T(8,128)(2,1)S(1)}, u32[]{:S(2)}, u32[]{:S(2)}) async-start(bf16[128,1,16,128]{3,2,1,0:T(8,128)(2,1)} %bitcast.125), calls=%async_computation.3 | async-start | bytes 1048576 | tf_op jit(solution)/shard_map/all_to_all | solution.py:287
  101.7 0.2 convolution_bitcast_fusion.13
  102.0 1.2 copy.324
  103.2 0.9 pad_maximum_fusion
  104.1 11.3 %all-to-all-done.3 = bf16[128,1,16,128]{3,2,1,0:T(8,128)(2,1)S(1)} async-done(((bf16[128,1,16,128]{3,2,1,0:T(8,128)(2,1)}), bf16[128,1,16,128]{3,2,1,0:T(8,128)(2,1)S(1)}, u32[]{:S(2)}, u32[]{:S(2)}) %all-to-all-start.3) | async-done | bytes 524320 | tf_op jit(solution)/shard_map/all_to_all | solution.py:287
  115.4 4.6 %all-to-all-start.1 = ((bf16[128,2,16,128]{3,2,1,0:T(8,128)(2,1)}), bf16[128,2,16,128]{3,2,1,0:T(8,128)(2,1)S(1)}, u32[]{:S(2)}, u32[]{:S(2)}) async-start(bf16[128,2,16,128]{3,2,1,0:T(8,128)(2,1)} %bitcast.237), calls=%async_computation.1 | async-start | bytes 2097152 | tf_op jit(solution)/shard_map/all_to_all | solution.py:250
  120.1 0.2 fusion.8
  120.4 1.9 broadcast_select_fusion.10
  122.2 1.3 scatter-add.69
  123.7 15.7 %all-to-all-done.1 = bf16[128,2,16,128]{3,2,1,0:T(8,128)(2,1)S(1)} async-done(((bf16[128,2,16,128]{3,2,1,0:T(8,128)(2,1)}), bf16[128,2,16,128]{3,2,1,0:T(8,128)(2,1)S(1)}, u32[]{:S(2)}, u32[]{:S(2)}) %all-to-all-start.1) | async-done | bytes 1048608 | tf_op jit(solution)/shard_map/all_to_all | solution.py:250
  139.7 0.2 convolution_bitcast_fusion
  139.9 0.2 convolution_bitcast_fusion.1
  140.1 0.2 convolution_bitcast_fusion.2
  140.4 0.2 convolution_bitcast_fusion.3
  140.6 0.2 convolution_bitcast_fusion.5
  140.8 0.2 convolution_bitcast_fusion.6
  141.1 0.2 convolution_bitcast_fusion.7
  141.3 0.2 convolution_bitcast_fusion.8
  141.5 0.9 pad_maximum_fusion.1
  142.5 0.6 convert_bitcast_fusion
  143.2 0.7 convolution_convert_fusion.5
  144.0 0.6 copy.285
  144.6 141.9 %all-reduce.45.cloned.1.call-done = (f32[3,3,128,128]{3,2,1,0:T(8,128)}, f32[3,3,128,128]{3,2,1,0:T(8,128)}) async-done(((f32[3,3,128,128]{3,2,1,0:T(8,128)}, f32[3,3,128,128]{3,2,1,0:T(8,128)}), (f32[3,3,128,128]{3,2,1,0:T(8,128)}, f32[3,3,128,128]{3,2,1,0:T(8,128)})) %all-reduce.45.cloned.1.call-update) | async-done | bytes 1179664 | tf_op jit(solution)/shard_map/psum | solution.py:298
  286.5 2.0 broadcast_multiply_fusion.1
  288.5 0.9 broadcast_multiply_fusion
  (288 shorter events, 4.8 us)
Async XLA Ops:
  7.2 60.1 %copy-start = (bf16[3,3,128,128]{3,2,1,0:T(8,128)(2,1)S(1)}, bf16[3,3,128,128]{3,2,1,0:T(8,128)(2,1)}, u32[]{:S(2)}) copy-start(bf16[3,3,128,128]{3,2,1,0:T(8,128)(2,1)} %param.40) | copy-start | bytes 884740
  12.0 12.4 %copy-start.1 = (bf16[1,16,16,128]{3,2,1,0:T(8,128)(2,1)S(1)}, bf16[1,16,16,128]{3,2,1,0:T(8,128)(2,1)}, u32[]{:S(2)}) copy-start(bf16[1,16,16,128]{3,2,1,0:T(8,128)(2,1)} %param.39) | copy-start | bytes 196612
  12.0 12.5 %copy-start.8 = (bf16[3,3,128,128]{3,2,1,0:T(8,128)(2,1)S(1)}, bf16[3,3,128,128]{3,2,1,0:T(8,128)(2,1)}, u32[]{:S(2)}) copy-start(bf16[3,3,128,128]{3,2,1,0:T(8,128)(2,1)} %param.41) | copy-start | bytes 884740
  12.9 44.2 %all-to-all-start = ((bf16[128,1,16,128]{3,2,1,0:T(8,128)(2,1)}), bf16[128,1,16,128]{3,2,1,0:T(8,128)(2,1)S(1)}, u32[]{:S(2)}, u32[]{:S(2)}) async-start(bf16[128,1,16,128]{3,2,1,0:T(8,128)(2,1)} %bitcast.8), calls=%async_computation | async-start | bytes 1048576 | tf_op jit(solution)/shard_map/all_to_all | solution.py:242
  24.4 1.2 copy-start.4
  24.5 1.2 copy-start.5
  53.9 2.5 copy-start.6
  53.9 2.5 copy-start.7
  57.1 9.9 %copy-start.2 = (bf16[1,16,16,128]{3,2,1,0:T(8,128)(2,1)S(1)}, bf16[1,16,16,128]{3,2,1,0:T(8,128)(2,1)}, u32[]{:S(2)}) copy-start(bf16[1,16,16,128]{3,2,1,0:T(8,128)(2,1)} %param.38) | copy-start | bytes 196612
  57.2 28.9 %all-to-all-start.2 = ((bf16[128,2,16,128]{3,2,1,0:T(8,128)(2,1)}), bf16[128,2,16,128]{3,2,1,0:T(8,128)(2,1)S(1)}, u32[]{:S(2)}, u32[]{:S(2)}) async-start(bf16[128,2,16,128]{3,2,1,0:T(8,128)(2,1)} %bitcast.231), calls=%async_computation.2 | async-start | bytes 2097152 | tf_op jit(solution)/shard_map/all_to_all | solution.py:266
  66.9 0.7 copy-start.10
  86.6 4.3 %copy-start.9 = (pred[8,3]{0,1:T(4,128)(4,1)S(1)}, pred[8,3]{0,1:T(4,128)(4,1)}, u32[]{:S(2)}) copy-start(pred[8,3]{0,1:T(4,128)(4,1)} %constant.670) | copy-start | bytes 76
  97.1 18.3 %all-to-all-start.3 = ((bf16[128,1,16,128]{3,2,1,0:T(8,128)(2,1)}), bf16[128,1,16,128]{3,2,1,0:T(8,128)(2,1)S(1)}, u32[]{:S(2)}, u32[]{:S(2)}) async-start(bf16[128,1,16,128]{3,2,1,0:T(8,128)(2,1)} %bitcast.125), calls=%async_computation.3 | async-start | bytes 1048576 | tf_op jit(solution)/shard_map/all_to_all | solution.py:287
  115.4 23.9 %all-to-all-start.1 = ((bf16[128,2,16,128]{3,2,1,0:T(8,128)(2,1)}), bf16[128,2,16,128]{3,2,1,0:T(8,128)(2,1)S(1)}, u32[]{:S(2)}, u32[]{:S(2)}) async-start(bf16[128,2,16,128]{3,2,1,0:T(8,128)(2,1)} %bitcast.237), calls=%async_computation.1 | async-start | bytes 2097152 | tf_op jit(solution)/shard_map/all_to_all | solution.py:250
  120.1 166.5 %all-reduce.45.cloned.1.call-start = ((), (), s32[]{:S(2)}) async-start(), calls=%async_computation.4 | async-start | bytes 2359296 | tf_op jit(solution)/shard_map/psum | solution.py:298
  286.5 2.0 copy-start.3
Sparse Core Ops, SparseCore 0:
  142.6 143.9 all-reduce.44
where the time goes:
time: 297 us; the launch traced here: 296 us
  waiting for transfers between devices  187 us (63%)
  between operations  40.9 us (14%)
  starting transfers between devices  30.5 us (10%)
  local copies, waits for them, and re-layouts  17.8 us (6%)
  other arithmetic  12.1 us (4%)
  matrix products  8.25 us (3%)
    psum x1, waiting for transfers between devices, local(): lax.psum((first_gradient_tilewise, second_gradient_tilewise), 'tile')  142 us
    all_to_all x1, waiting for transfers between devices, local(): lax.all_to_all(for_sending(sent_back_hidden), 'tile', split_axis=0, conca...  17.7 us
    all_to_all x1, waiting for transfers between devices, local(): lax.all_to_all(dispatched_hidden, 'tile', split_axis=0, concat_axis=0, ti...  15.7 us
    all_to_all x1, starting transfers between devices, local(): lax.all_to_all(dispatched_input, 'tile', split_axis=0, concat_axis=0, til...  11.5 us
    all_to_all x1, waiting for transfers between devices, local(): lax.all_to_all(for_sending(sent_back_input), 'tile', split_axis=0, concat...  11.3 us
    all_to_all x1, starting transfers between devices, local(): lax.all_to_all(for_sending(sent_back_hidden), 'tile', split_axis=0, conca...  9.76 us
  transfers between devices with their start and end apart: 5, of which 4 were waited for; matrix products, arithmetic and copies ran while one was open for 5% of the time, Pallas kernels for 0%

commit v1 on v0

v1 whole, which is shorter than its diff:
```python
import functools
import math

import jax
import jax.numpy as jnp
import numpy as np
from jax import lax
from jax.experimental import pallas as pl
from jax.experimental.pallas import tpu as pltpu
from jax.sharding import PartitionSpec as P

SIDE = 16
PX = SIDE * SIDE
CH = 128
TILES = 128
FIRST, SECOND = 1, 2
SCALE = 1.0 / math.sqrt(TILES * PX)

gelu_scale = 0.7978845608028654
gelu_cubic = 0.044715

F32, BF16 = jnp.float32, jnp.bfloat16
MESH = pl.DeviceIdType.MESH

STRIDE = {"y": 32, "x": 8, "z": 2}
SHIFT = {"y": 5, "x": 3, "z": 1}
PLANS = (("x", "y", "z"), ("y", "z", "x"), ("z", "x", "y"))
LAYER_PLAN = (0, 1, 2, 0, 2, 1)

ROW_STEP = (-1, -1, 0, 1, 1, 1, 0, -1)
COL_STEP = (0, 1, 1, 1, 0, -1, -1, -1)

LAYER_ROWS = 80


def side_pixel(j, depth, along):
    last = SIDE - 1
    return ((depth, along), (along, last - depth), (last - depth, last - along), (last - along, depth))[j]


def layer_rows(width):
    for q in range(5):
        for e in range(4):
            for j in range(4):
                row = q * 16 + e * 4 + j
                if q < 4:
                    yield row, 2 * j, 4 * q + e
                elif 2 - width <= e < 2:
                    yield row, 2 * j + 1, SIDE - 2 + e


def rim_place(d, depth, along, width):
    facing = (d + 4) % 8
    i, j = side_pixel(facing // 2, depth, along)
    return width + SIDE * ROW_STEP[d] + i, width + SIDE * COL_STEP[d] + j


def pick_matrix(depth):
    out = np.zeros((LAYER_ROWS, PX), np.float32)
    for row, compass, along in layer_rows(2):
        i, j = side_pixel(compass // 2, depth, along)
        out[row, i * SIDE + j] = 1
    return out


def shift_matrix(width):
    rows = SIDE + 2 * width
    out = np.zeros((3, rows, SIDE, PX), np.float32)
    for b in range(3):
        for i in range(SIDE):
            for j in range(SIDE):
                src = j + b * width - width
                if 0 <= src < SIDE:
                    out[b, i + width, j, i * SIDE + src] = 1
    return out.reshape(3 * rows * SIDE, PX)


def rim_matrix(width):
    rows = SIDE + 2 * width
    out = np.zeros((3, rows, SIDE, width * LAYER_ROWS), np.float32)
    for depth in range(width):
        for row, d, along in layer_rows(width):
            i, j = rim_place(d, depth, along, width)
            for b in range(3):
                col = j - b * width
                if 0 <= col < SIDE:
                    out[b, i, col, depth * LAYER_ROWS + row] = 1
    return out.reshape(3 * rows * SIDE, width * LAYER_ROWS)


def taps_matrix(width):
    out = np.zeros((3, 3, width * LAYER_ROWS, PX), np.float32)
    for depth in range(width):
        for row, d, along in layer_rows(width):
            i, j = rim_place(d, depth, along, width)
            for a in range(3):
                for b in range(3):
                    si, sj = i - width * (2 - a), j - width * (2 - b)
                    if 0 <= si < SIDE and 0 <= sj < SIDE:
                        out[a, b, depth * LAYER_ROWS + row, si * SIDE + sj] = 1
    return out.reshape(9 * width * LAYER_ROWS, PX)


def constants():
    pick = np.concatenate([pick_matrix(0), pick_matrix(1)])
    arrays = (
        pick,
        np.ascontiguousarray(pick.T),
        shift_matrix(1),
        shift_matrix(2),
        rim_matrix(1),
        rim_matrix(2),
        taps_matrix(1),
        taps_matrix(2),
    )
    return [jnp.asarray(a, BF16) for a in arrays]


def dot(a, b):
    return jnp.dot(a, b, preferred_element_type=F32)


def dot_first(a, b):
    return lax.dot_general(a, b, (((0,), (0,)), ((), ())), preferred_element_type=F32)


def coordinate(index, axis):
    return (index >> SHIFT[axis]) & 3


def block_kernel(
    feat, cot, k1, k2, nb, turns,
    pick, spread, shift1, shift2, rim1, rim2, taps1, taps2,
    out, fgrad, g1_out, g2_out,
    buf, msg, recv, choose, kt1, kt2, x1f, x1g, x2h, x2c, zcat, center, mid, deriv,
    grads, core_in, part, rs_in, z_in, ag_in, sib_in,
    send_sem, recv_sem, ar_send, ar_recv,
):
    me = lax.axis_index("tile")
    core = me & 1
    pos = {axis: coordinate(me, axis) for axis in "yxz"}

    def along(axis, i):
        return me + (((pos[axis] + i) & 3) - pos[axis]) * STRIDE[axis]

    def plane_peers():
        for dy in range(4):
            for dx in range(4):
                if dy or dx:
                    y, x = (pos["y"] + dy) & 3, (pos["x"] + dx) & 3
                    yield me + (y - pos["y"]) * STRIDE["y"] + (x - pos["x"]) * STRIDE["x"], y * 4 + x

    sibling = me + 1 - 2 * core

    peers = [sibling] + [device for device, _ in plane_peers()]
    for axis in "yxz":
        for i in range(1, 4):
            if axis == "z":
                peers.append(along(axis, i))
            peers.append(along(axis, i) + 1 - 2 * core)
    barrier = pltpu.get_barrier_semaphore()
    for device in peers:
        pl.semaphore_signal(barrier, inc=1, device_id=(device,), device_id_type=MESH)

    def remote(src, dst, send, arrive, device):
        pltpu.make_async_remote_copy(
            src_ref=src, dst_ref=dst, send_sem=send, recv_sem=arrive, device_id=(device,), device_id_type=MESH
        ).start()

    def wait_bytes(ref, sem):
        pltpu.make_async_copy(ref, ref, sem).wait()

    def own_rows(layer):
        a, b, _ = PLANS[LAYER_PLAN[layer]]
        return pl.ds(pl.multiple_of((pos[b] * 4 + pos[a]) * 16, 16), 16)

    def put(layer, values):
        buf[layer, :, own_rows(layer), :] = values.astype(BF16).reshape(5, 16, CH)

    def send_a(layer):
        axis = PLANS[LAYER_PLAN[layer]][0]
        view = buf.at[layer, :, own_rows(layer), :]
        for i in range(1, 4):
            remote(view, view, send_sem.at[layer, 0], recv_sem.at[layer, 0], along(axis, i))

    def send_b(layer):
        axis = PLANS[LAYER_PLAN[layer]][1]
        wait_bytes(buf.at[layer, :, pl.ds(0, 48), :], recv_sem.at[layer, 0])
        view = buf.at[layer, :, pl.ds(pl.multiple_of(pos[axis] * 64, 64), 64), :]
        for i in range(1, 4):
            remote(view, view, send_sem.at[layer, 1], recv_sem.at[layer, 1], along(axis, i))

    def send_line(layer, chooser):
        axis = PLANS[LAYER_PLAN[layer]][2]
        wait_bytes(buf.at[layer, :, pl.ds(0, 192), :], recv_sem.at[layer, 1])
        for q in range(5):
            msg[layer, q] = dot(choose[chooser, 0 if q < 4 else 1], buf[layer, q]).astype(BF16)
        mine = pl.ds(pl.multiple_of((pos[axis] * 2 + core) * 16, 16), 16)
        for i in range(4):
            for flip in range(2):
                if i or flip:
                    other = core + flip - 2 * core * flip
                    device = along(axis, i) - core + other
                    theirs = pl.ds(pl.multiple_of((((pos[axis] + i) & 3) * 2 + other) * 16, 16), 16)
                    remote(
                        msg.at[layer, :, theirs, :], recv.at[layer, :, mine, :],
                        send_sem.at[layer, 2], recv_sem.at[layer, 2], device,
                    )
        recv[layer, :, mine, :] = msg[layer, :, mine, :]

    def arrived(layer):
        wait_bytes(recv.at[layer, :, pl.ds(0, 112), :], recv_sem.at[layer, 2])
        total = recv[layer, :, 0:16, :].astype(F32)
        for g in range(1, 8):
            total += recv[layer, :, g * 16 : g * 16 + 16, :].astype(F32)
        return total.reshape(LAYER_ROWS, CH)

    def finish_sends(layer):
        wait_bytes(buf.at[layer, :, pl.ds(0, 48), :], send_sem.at[layer, 0])
        wait_bytes(buf.at[layer, :, pl.ds(0, 192), :], send_sem.at[layer, 1])
        wait_bytes(recv.at[layer, :, pl.ds(0, 112), :], send_sem.at[layer, 2])

    def table_rows(device_of_row, column_of_row):
        rows = device_of_row.shape[0]
        ids = lax.broadcasted_iota(jnp.int32, (rows, TILES), 1)
        hot = jnp.where(ids == device_of_row, 1.0, 0.0).astype(BF16)
        keep = lax.broadcasted_iota(jnp.int32, (rows, 8), 1) == column_of_row
        picked = []
        for table in (nb, turns):
            values = dot(hot, table[...].astype(F32).astype(BF16))
            values = jnp.sum(jnp.where(keep, values, 0.0), axis=1, keepdims=True)
            picked.append(values.astype(jnp.int32))
        return picked

    def build_forward(slot, plan):
        a, b, line = PLANS[plan]
        row = lax.broadcasted_iota(jnp.int32, (128, 1), 0)
        dest = me - core - pos[line] * STRIDE[line] + (row >> 5) * STRIDE[line] + ((row >> 4) & 1)
        e, j = (row >> 2) & 3, row & 3
        for corner in range(2):
            source, quarter = table_rows(dest, 2 * j + corner)
            here = (source >= 0) & (coordinate(source, line) == pos[line]) & ((source & 1) == core)
            place = (coordinate(source, b) * 4 + coordinate(source, a)) * 16 + e * 4 + ((j + 2 + quarter) & 3)
            place = jnp.where(here, place, -1)
            lanes = lax.broadcasted_iota(jnp.int32, (128, PX), 1)
            choose[slot, corner] = jnp.where(lanes == place, 1.0, 0.0).astype(BF16)

    def build_adjoint(slot, plan):
        a, b, line = PLANS[plan]
        row = lax.broadcasted_iota(jnp.int32, (PX, 1), 0)
        owner = (
            me - pos[a] * STRIDE[a] - pos[b] * STRIDE[b]
            + (row >> 6) * STRIDE[b] + ((row >> 4) & 3) * STRIDE[a]
        )
        e, j = (row >> 2) & 3, row & 3
        for corner in range(2):
            target, quarter = table_rows(owner, 2 * j + corner)
            here = (target >= 0) & (coordinate(target, a) == pos[a]) & (coordinate(target, b) == pos[b])
            place = (coordinate(target, line) * 2 + (target & 1)) * 16 + e * 4 + ((j + 2 + quarter) & 3)
            place = jnp.where(here, place, -1)
            lanes = lax.broadcasted_iota(jnp.int32, (PX, 128), 1)
            choose[slot, corner] = jnp.where(lanes == place, 1.0, 0.0).T.astype(BF16)

    def flip_kernel(kernel, dest):
        for a in range(3):
            for b in range(3):
                tap = kernel[2 - a, (2 - b) * CH : (3 - b) * CH, :]
                at = (a * 3 + b) * CH
                dest[at : at + CH, :] = tap.astype(F32).T.astype(BF16)

    def lay(dest, columns):
        rows = dest.shape[0]
        for b in range(3):
            dest[:, b * CH : (b + 1) * CH] = columns[b * rows : (b + 1) * rows].astype(BF16)

    def conv(x, kernel, dilation):
        total = None
        for a in range(3):
            window = x[a * dilation * SIDE : a * dilation * SIDE + PX, :]
            tap = dot(window, kernel(a))
            total = tap if total is None else total + tap
        return total

    def rim_gradient(values, taps, kernel_t, width):
        rows = width * LAYER_ROWS
        for tap in range(9):
            shifted = dot(taps[tap * rows : (tap + 1) * rows, :], values)
            zcat[0:rows, tap * CH : (tap + 1) * CH] = shifted.astype(BF16)
        return dot(zcat[0:rows, :], kernel_t[...])

    def kernel_gradient(which, x, right, dilation):
        for a in range(3):
            window = x[a * dilation * SIDE : a * dilation * SIDE + PX, :]
            grads[which, a * 3 * CH : (a + 1) * 3 * CH, :] = dot_first(window, right)

    half = pl.multiple_of(core * 32, 8)
    other_half = pl.multiple_of(32 - core * 32, 8)
    owner = pos["y"] * 4 + pos["x"]

    def ar_core(which):
        for i in range(16):
            remote(
                grads.at[which, pl.ds(pl.multiple_of(i * 72 + other_half, 8), 40), :], core_in.at[which, i],
                ar_send.at[which, 0], ar_recv.at[which, 0], sibling,
            )

    def ar_scatter(which):
        wait_bytes(core_in.at[which], ar_recv.at[which, 0])
        for i in range(16):
            mine = grads[which, pl.ds(pl.multiple_of(i * 72 + half, 8), 40), :]
            part[which, i] = mine + core_in[which, i]
        for device, i in plane_peers():
            remote(part.at[which, i], rs_in.at[which, owner], ar_send.at[which, 1], ar_recv.at[which, 1], device)
        rs_in[which, owner] = part[which, owner]

    def ar_line(which):
        wait_bytes(rs_in.at[which, pl.ds(0, 15)], ar_recv.at[which, 1])
        total = rs_in[which, 0]
        for i in range(1, 16):
            total += rs_in[which, i]
        z_in[which, pos["z"]] = total
        for i in range(1, 4):
            remote(
                z_in.at[which, pos["z"]], z_in.at[which, pos["z"]],
                ar_send.at[which, 2], ar_recv.at[which, 2], along("z", i),
            )

    def ar_gather(which):
        wait_bytes(z_in.at[which, pl.ds(0, 3)], ar_recv.at[which, 2])
        total = ((z_in[which, 0] + z_in[which, 1]) + z_in[which, 2]) + z_in[which, 3]
        ag_in[which, owner] = total * SCALE
        for device, _ in plane_peers():
            remote(
                ag_in.at[which, owner], ag_in.at[which, owner],
                ar_send.at[which, 3], ar_recv.at[which, 3], device,
            )

    def ar_share(which):
        wait_bytes(ag_in.at[which, pl.ds(0, 15)], ar_recv.at[which, 3])
        remote(ag_in.at[which], sib_in.at[which], ar_send.at[which, 4], ar_recv.at[which, 4], sibling)

    def ar_finish(which, dest):
        wait_bytes(sib_in.at[which], ar_recv.at[which, 4])
        first = core == 0
        for i in range(16):
            mine, theirs = ag_in[which, i], sib_in[which, i]
            dest[i * 72 : i * 72 + 40, :] = jnp.where(first, mine, theirs)
            dest[i * 72 + 40 : i * 72 + 72, :] = jnp.where(first, theirs, mine)[8:40]
        wait_bytes(core_in.at[which], ar_send.at[which, 0])
        wait_bytes(rs_in.at[which, pl.ds(0, 15)], ar_send.at[which, 1])
        wait_bytes(z_in.at[which, pl.ds(0, 3)], ar_send.at[which, 2])
        wait_bytes(ag_in.at[which, pl.ds(0, 15)], ar_send.at[which, 3])
        wait_bytes(sib_in.at[which], ar_send.at[which, 4])

    put(0, dot(pick[0:LAYER_ROWS, :], feat[...]))
    flip_kernel(k2, kt2)
    rim = rim_gradient(cot[...], taps2, kt2, SECOND)
    put(1, rim[0:LAYER_ROWS])
    put(2, rim[LAYER_ROWS : 2 * LAYER_ROWS])
    pl.semaphore_wait(barrier, len(peers))
    for layer in range(3):
        send_a(layer)
    build_forward(0, 0)
    build_adjoint(1, 1)
    build_adjoint(2, 2)
    for layer in range(3):
        send_b(layer)
    center[0 : 3 * 288, :] = dot(shift1[...], feat[...])
    lay(x2c, dot(shift2[...], cot[...]))
    mid[...] = conv(x2c, lambda a: kt2[a * 384 : (a + 1) * 384, :], SECOND).astype(BF16)
    for layer in range(3):
        send_line(layer, layer)
    flip_kernel(k1, kt1)
    build_forward(3, 2)

    lay(x1f, center[0 : 3 * 288, :] + dot(rim1[...], arrived(0).astype(BF16)))
    v = conv(x1f, lambda a: k1[a], FIRST)
    tangent = jnp.tanh(gelu_scale * (v + gelu_cubic * v * v * v))
    hidden = (0.5 * v * (1.0 + tangent)).astype(BF16)
    deriv[...] = 0.5 * (1.0 + tangent) + 0.5 * v * (1.0 - tangent * tangent) * gelu_scale * (
        1.0 + 3.0 * gelu_cubic * v * v
    )
    rows = dot(pick[...], hidden)
    put(3, rows[0:LAYER_ROWS])
    put(4, rows[LAYER_ROWS : 2 * LAYER_ROWS])
    send_a(3)
    send_a(4)

    sums = jnp.concatenate([arrived(1), arrived(2)], axis=0)
    high = sums.astype(BF16)
    low = (sums - high.astype(F32)).astype(BF16)
    grad_hidden = mid[...].astype(F32) + dot(spread[...], high) + dot(spread[...], low)
    gpre = (grad_hidden * deriv[...]).astype(BF16)
    put(5, rim_gradient(gpre, taps1, kt1, FIRST))
    send_a(5)
    kernel_gradient(0, x1f, gpre, FIRST)
    ar_core(0)
    send_b(3)
    send_b(4)
    center[...] = dot(shift2[...], hidden)
    send_b(5)
    lay(x1g, dot(shift1[...], gpre))
    mid[...] = conv(x1g, lambda a: kt1[a * 384 : (a + 1) * 384, :], FIRST).astype(BF16)
    ar_scatter(0)
    send_line(3, 0)
    send_line(4, 3)
    send_line(5, 1)
    ar_line(0)

    rims = jnp.concatenate([arrived(3), arrived(4)], axis=0).astype(BF16)
    lay(x2h, center[...] + dot(rim2[...], rims))
    kernel_gradient(1, x2h, cot[...], SECOND)
    ar_core(1)
    out[...] = conv(x2h, lambda a: k2[a], SECOND).astype(BF16)
    ar_gather(0)
    ar_scatter(1)
    sums = arrived(5)
    high = sums.astype(BF16)
    low = (sums - high.astype(F32)).astype(BF16)
    fgrad[...] = (
        mid[...].astype(F32) + dot(spread[:, 0:LAYER_ROWS], high) + dot(spread[:, 0:LAYER_ROWS], low)
    ).astype(BF16)
    ar_share(0)
    ar_line(1)
    ar_finish(0, g1_out)
    ar_gather(1)
    for layer in range(6):
        finish_sends(layer)
    ar_share(1)
    ar_finish(1, g2_out)


def local(features, cotangent, kernel_first_layer, kernel_second_layer, neighbors, turns):
    vmem = pl.BlockSpec(memory_space=pltpu.VMEM)
    operands = [
        features.reshape(PX, CH),
        cotangent.reshape(PX, CH),
        kernel_first_layer.reshape(3, 3 * CH, CH),
        kernel_second_layer.reshape(3, 3 * CH, CH),
        neighbors,
        turns,
    ] + constants()
    output, features_gradient, first, second = pl.pallas_call(
        block_kernel,
        out_shape=(
            jax.ShapeDtypeStruct((PX, CH), BF16),
            jax.ShapeDtypeStruct((PX, CH), BF16),
            jax.ShapeDtypeStruct((9 * CH, CH), F32),
            jax.ShapeDtypeStruct((9 * CH, CH), F32),
        ),
        in_specs=[vmem] * len(operands),
        out_specs=(vmem,) * 4,
        scratch_shapes=[
            pltpu.VMEM((6, 5, 256, CH), BF16),
            pltpu.VMEM((6, 5, 128, CH), BF16),
            pltpu.VMEM((6, 5, 128, CH), BF16),
            pltpu.VMEM((4, 2, 128, PX), BF16),
            pltpu.VMEM((9 * CH, CH), BF16),
            pltpu.VMEM((9 * CH, CH), BF16),
            pltpu.VMEM((288, 3 * CH), BF16),
            pltpu.VMEM((288, 3 * CH), BF16),
            pltpu.VMEM((320, 3 * CH), BF16),
            pltpu.VMEM((320, 3 * CH), BF16),
            pltpu.VMEM((2 * LAYER_ROWS, 9 * CH), BF16),
            pltpu.VMEM((3 * 320, CH), F32),
            pltpu.VMEM((PX, CH), BF16),
            pltpu.VMEM((PX, CH), F32),
            pltpu.VMEM((2, 9 * CH, CH), F32),
            pltpu.VMEM((2, 16, 40, CH), F32),
            pltpu.VMEM((2, 16, 40, CH), F32),
            pltpu.VMEM((2, 16, 40, CH), F32),
            pltpu.VMEM((2, 4, 40, CH), F32),
            pltpu.VMEM((2, 16, 40, CH), F32),
            pltpu.VMEM((2, 16, 40, CH), F32),
            pltpu.SemaphoreType.DMA((6, 3)),
            pltpu.SemaphoreType.DMA((6, 3)),
            pltpu.SemaphoreType.DMA((2, 5)),
            pltpu.SemaphoreType.DMA((2, 5)),
        ],
        compiler_params=pltpu.CompilerParams(
            collective_id=0, has_side_effects=True, vmem_limit_bytes=48 * 2**20
        ),
    )(*operands)
    return (
        output.reshape(features.shape),
        features_gradient.reshape(features.shape),
        first.reshape(kernel_first_layer.shape),
        second.reshape(kernel_second_layer.shape),
    )


def solution(mesh):
    placed = (P("tile", None, None, None), P("tile", None, None, None), P(), P(), P(), P())
    return jax.shard_map(
        local,
        mesh=mesh,
        in_specs=placed,
        out_specs=(P("tile", None, None, None), P("tile", None, None, None), P(), P()),
        check_vma=False,
    )
```

time: 297 us -> 78 us (0.26)
  waiting for transfers between devices: 187 us -> 0 us
  Pallas kernels: 0 us -> 61.6 us
  between operations: 40.9 us -> 0.67 us
  starting transfers between devices: 30.5 us -> 0 us
  other arithmetic: 12.1 us -> 0 us
  matrix products: 8.25 us -> 0 us
    psum x1 -> x0, waiting for transfers between devices: 142 us -> none  [local(): lax.psum((first_gradient_tilewise, second_gradient_tilewise), 'tile')]
    pallas_call x0 -> x1, Pallas kernels: none -> 61.6 us  [local(): pl.pallas_call(block_kernel, out_shape=(jax.ShapeDtypeStruct((PX, CH), BF...]
    all_to_all x4 -> x0, waiting for transfers between devices: 44.7 us -> none  [the longest x1 17.7 us: local(): lax.all_to_all(for_sending(sent_back_hidden), 'tile', split_axis=0, conca...]
    all_to_all x4 -> x0, starting transfers between devices: 30.5 us -> none  [the longest x1 11.5 us: local(): lax.all_to_all(dispatched_input, 'tile', split_axis=0, concat_axis=0, til...]
    unnamed x59 -> x30, local copies, waits for them, and re-layouts: 5.48 us -> 15.1 us
    another operation x13 -> x0, other arithmetic: 6.37 us -> none
    dot_general x24 -> x0, matrix products: 5.64 us -> none  [the longest x18 3.57 us: kernel_gradient_fn(): lax.dot_general(window, flat_cot, (((0,), (0,)), ((), ())), preferred_ele...]
    slice x32 -> x0, local copies, waits for them, and re-layouts: 3.98 us -> none  [the longest x6 2.3 us: strip_of(): return strip_block[..., row_pick, col_pick, :]]
  transfers between devices with their start and end apart: 5 -> 0, of which waited for: 4 -> 0; matrix products, arithmetic and copies ran while one was open for 5% -> 0% of each run, Pallas kernels for 0% -> 0%
where the time goes in v1:
time: 78 us; the launch traced here: 77.4 us
  Pallas kernels  61.6 us (79%)
  local copies, waits for them, and re-layouts  15.1 us (19%)
    pallas_call x1, Pallas kernels, local(): pl.pallas_call(block_kernel, out_shape=(jax.ShapeDtypeStruct((PX, CH), BF...  61.6 us
    unnamed x30, local copies, waits for them, and re-layouts  15.1 us

profile of v1, /device:TPU:1, one launch (start us, length us, event | category | flops | bytes accessed | tf_op | source)
XLA Modules:
  0.0 77.4 jit_solution(1562172379244508122)
XLA Ops:
  0.6 0.0 copy-start.8
  0.6 0.8 %copy.18.nb = s32[128,8]{1,0:T(8,128)S(1)} copy(s32[128,8]{0,1:T(8,128)} %param.18) | data formatting | bytes 8192 | tf_op args[4]
  1.5 0.8 %copy.19.turns = s32[128,8]{1,0:T(8,128)S(1)} copy(s32[128,8]{0,1:T(8,128)} %param.19) | data formatting | bytes 8192 | tf_op args[5]
  2.3 0.0 copy-done.8
  2.3 0.0 copy-start
  2.3 1.1 %copy-done = bf16[1440,256]{1,0:T(8,128)(2,1)S(1)} copy-done((bf16[1440,256]{1,0:T(8,128)(2,1)S(1)}, bf16[1440,256]{1,0:T(8,128)(2,1)}, u32[]{:S(2)}) %copy-start) | copy-done | bytes 737304
  3.4 0.0 copy-start.1
  3.4 1.0 %copy-done.1 = bf16[960,160]{1,0:T(8,128)(2,1)S(1)} copy-done((bf16[960,160]{1,0:T(8,128)(2,1)S(1)}, bf16[960,160]{1,0:T(8,128)(2,1)}, u32[]{:S(2)}) %copy-start.1) | copy-done | bytes 307224
  4.4 0.0 copy-start.2
  4.4 1.0 %copy-done.2 = bf16[960,256]{1,0:T(8,128)(2,1)S(1)} copy-done((bf16[960,256]{1,0:T(8,128)(2,1)S(1)}, bf16[960,256]{1,0:T(8,128)(2,1)}, u32[]{:S(2)}) %copy-start.2) | copy-done | bytes 491544
  5.4 0.0 copy-start.3
  5.4 1.0 %copy-done.3 = bf16[864,256]{1,0:T(8,128)(2,1)S(1)} copy-done((bf16[864,256]{1,0:T(8,128)(2,1)S(1)}, bf16[864,256]{1,0:T(8,128)(2,1)}, u32[]{:S(2)}) %copy-start.3) | copy-done | bytes 442392
  6.5 0.0 copy-start.4
  6.5 1.0 %copy-done.4 = bf16[720,256]{1,0:T(8,128)(2,1)S(1)} copy-done((bf16[720,256]{1,0:T(8,128)(2,1)S(1)}, bf16[720,256]{1,0:T(8,128)(2,1)}, u32[]{:S(2)}) %copy-start.4) | copy-done | bytes 368664
  7.4 0.0 copy-start.5
  7.4 1.0 %copy-done.5 = bf16[3,3,128,128]{3,2,1,0:T(8,128)(2,1)S(1)} copy-done((bf16[3,3,128,128]{3,2,1,0:T(8,128)(2,1)S(1)}, bf16[3,3,128,128]{3,2,1,0:T(8,128)(2,1)}, u32[]{:S(2)}) %copy-start.5) | copy-done | bytes 294936
  8.4 0.0 copy-start.6
  8.4 1.0 %copy-done.6 = bf16[3,3,128,128]{3,2,1,0:T(8,128)(2,1)S(1)} copy-done((bf16[3,3,128,128]{3,2,1,0:T(8,128)(2,1)S(1)}, bf16[3,3,128,128]{3,2,1,0:T(8,128)(2,1)}, u32[]{:S(2)}) %copy-start.6) | copy-done | bytes 294936
  9.4 0.0 copy-start.7
  9.4 0.9 %copy-done.7 = bf16[864,80]{1,0:T(8,128)(2,1)S(1)} copy-done((bf16[864,80]{1,0:T(8,128)(2,1)S(1)}, bf16[864,80]{1,0:T(8,128)(2,1)}, u32[]{:S(2)}) %copy-start.7) | copy-done | bytes 138264
  10.3 0.0 copy-start.9
  10.3 0.9 %copy-done.9 = bf16[160,256]{1,0:T(8,128)(2,1)S(1)} copy-done((bf16[160,256]{1,0:T(8,128)(2,1)S(1)}, bf16[160,256]{1,0:T(8,128)(2,1)}, u32[]{:S(2)}) %copy-start.9) | copy-done | bytes 81944
  11.2 0.0 copy-start.10
  11.2 0.8 %copy-done.10 = bf16[1,16,16,128]{3,2,1,0:T(8,128)(2,1)S(1)} copy-done((bf16[1,16,16,128]{3,2,1,0:T(8,128)(2,1)S(1)}, bf16[1,16,16,128]{3,2,1,0:T(8,128)(2,1)}, u32[]{:S(2)}) %copy-start.10) | copy-done | bytes 65560
  12.0 0.0 copy-start.11
  12.0 0.8 %copy-done.11 = bf16[1,16,16,128]{3,2,1,0:T(8,128)(2,1)S(1)} copy-done((bf16[1,16,16,128]{3,2,1,0:T(8,128)(2,1)S(1)}, bf16[1,16,16,128]{3,2,1,0:T(8,128)(2,1)}, u32[]{:S(2)}) %copy-start.11) | copy-done | bytes 65560
  12.9 61.6 %shard_map.165 = (bf16[256,128]{1,0:T(8,128)(2,1)S(1)}, bf16[256,128]{1,0:T(8,128)(2,1)S(1)}, f32[1152,128]{1,0:T(8,128)S(1)}, f32[1152,128]{1,0:T(8,128)S(1)}) custom-call(bf16[256,128]{1,0:T(8,128)(2,1)S(1)} %bitcast.14, bf16[256,128]{1,0:T(8,128)(2,1)S(1)} %bitcast.15, bf16[3,384,128]{2,1,0:T(8,128)(2,1)S(1)} %bitcast.10, ...), custom_call_target="tpu_custom_call" | custom-call | tf_op jit(solution)/shard_map/pallas_call | solution.py:443
  74.5 0.6 copy.24
  75.1 0.6 copy.25
  75.8 0.8 %copy.26 = f32[3,3,128,128]{3,2,1,0:T(8,128)} copy(f32[3,3,128,128]{3,2,1,0:T(8,128)S(1)} %bitcast.9) | data formatting | bytes 1179648
  76.6 0.8 %copy.27 = f32[3,3,128,128]{3,2,1,0:T(8,128)} copy(f32[3,3,128,128]{3,2,1,0:T(8,128)S(1)} %bitcast.8) | data formatting | bytes 1179648
Async XLA Ops:
  0.6 1.6 %copy-start.8 = (bf16[256,160]{1,0:T(8,128)(2,1)S(1)}, bf16[256,160]{1,0:T(8,128)(2,1)}, u32[]{:S(2)}) copy-start(bf16[256,160]{1,0:T(8,128)(2,1)} %constant.17.clone.spread) | copy-start | bytes 245764
  2.3 1.1 %copy-start = (bf16[1440,256]{1,0:T(8,128)(2,1)S(1)}, bf16[1440,256]{1,0:T(8,128)(2,1)}, u32[]{:S(2)}) copy-start(bf16[1440,256]{1,0:T(8,128)(2,1)} %constant.23.clone.taps2) | copy-start | bytes 2211844
  3.4 1.0 %copy-start.1 = (bf16[960,160]{1,0:T(8,128)(2,1)S(1)}, bf16[960,160]{1,0:T(8,128)(2,1)}, u32[]{:S(2)}) copy-start(bf16[960,160]{1,0:T(8,128)(2,1)} %constant.21.clone.rim2) | copy-start | bytes 921604
  4.4 1.0 %copy-start.2 = (bf16[960,256]{1,0:T(8,128)(2,1)S(1)}, bf16[960,256]{1,0:T(8,128)(2,1)}, u32[]{:S(2)}) copy-start(bf16[960,256]{1,0:T(8,128)(2,1)} %constant.19.clone.shift2) | copy-start | bytes 1474564
  5.4 1.0 %copy-start.3 = (bf16[864,256]{1,0:T(8,128)(2,1)S(1)}, bf16[864,256]{1,0:T(8,128)(2,1)}, u32[]{:S(2)}) copy-start(bf16[864,256]{1,0:T(8,128)(2,1)} %constant.18.clone.shift1) | copy-start | bytes 1327108
  6.5 1.0 %copy-start.4 = (bf16[720,256]{1,0:T(8,128)(2,1)S(1)}, bf16[720,256]{1,0:T(8,128)(2,1)}, u32[]{:S(2)}) copy-start(bf16[720,256]{1,0:T(8,128)(2,1)} %constant.22.clone.taps1) | copy-start | bytes 1105924
  7.4 1.0 %copy-start.5 = (bf16[3,3,128,128]{3,2,1,0:T(8,128)(2,1)S(1)}, bf16[3,3,128,128]{3,2,1,0:T(8,128)(2,1)}, u32[]{:S(2)}) copy-start(bf16[3,3,128,128]{3,2,1,0:T(8,128)(2,1)} %param.16) | copy-start | bytes 884740
  8.4 1.0 %copy-start.6 = (bf16[3,3,128,128]{3,2,1,0:T(8,128)(2,1)S(1)}, bf16[3,3,128,128]{3,2,1,0:T(8,128)(2,1)}, u32[]{:S(2)}) copy-start(bf16[3,3,128,128]{3,2,1,0:T(8,128)(2,1)} %param.17) | copy-start | bytes 884740
  9.4 0.9 %copy-start.7 = (bf16[864,80]{1,0:T(8,128)(2,1)S(1)}, bf16[864,80]{1,0:T(8,128)(2,1)}, u32[]{:S(2)}) copy-start(bf16[864,80]{1,0:T(8,128)(2,1)} %constant.20.clone.rim1) | copy-start | bytes 414724
  10.3 0.9 %copy-start.9 = (bf16[160,256]{1,0:T(8,128)(2,1)S(1)}, bf16[160,256]{1,0:T(8,128)(2,1)}, u32[]{:S(2)}) copy-start(bf16[160,256]{1,0:T(8,128)(2,1)} %constant.16.clone.pick) | copy-start | bytes 245764
  11.2 0.8 %copy-start.10 = (bf16[1,16,16,128]{3,2,1,0:T(8,128)(2,1)S(1)}, bf16[1,16,16,128]{3,2,1,0:T(8,128)(2,1)}, u32[]{:S(2)}) copy-start(bf16[1,16,16,128]{3,2,1,0:T(8,128)(2,1)} %param.14) | copy-start | bytes 196612
  12.0 0.8 %copy-start.11 = (bf16[1,16,16,128]{3,2,1,0:T(8,128)(2,1)S(1)}, bf16[1,16,16,128]{3,2,1,0:T(8,128)(2,1)}, u32[]{:S(2)}) copy-start(bf16[1,16,16,128]{3,2,1,0:T(8,128)(2,1)} %param.15) | copy-start | bytes 196612

commit v2 on v1

--- a/solution.py
+++ b/solution.py
@@ -26,11 +26,19 @@
 SHIFT = {"y": 5, "x": 3, "z": 1}
 PLANS = (("x", "y", "z"), ("y", "z", "x"), ("z", "x", "y"))
 LAYER_PLAN = (0, 1, 2, 0, 2, 1)
+LAYERS = 6
+SLICES = (4, 4, 4, 4, 4, 5)
+CORNER_SLICE = (3, 0, 0, 3, 3, 4)
 
 ROW_STEP = (-1, -1, 0, 1, 1, 1, 0, -1)
 COL_STEP = (0, 1, 1, 1, 0, -1, -1, -1)
 
 LAYER_ROWS = 80
+
+FAR_FIRST = (2, 1, 3)
+
+CHUNK, HALF = 72, 48
+SUM_PLANS = (("z", "x", "y"), ("x", "y", "z"))
 
 
 def side_pixel(j, depth, along):
@@ -101,6 +109,30 @@
     return out.reshape(9 * width * LAYER_ROWS, PX)
 
 
+SIDE_TAP = ((0, 1), (1, 2), (2, 1), (1, 0))
+CORNER_TAP = ((0, 2), (2, 2), (2, 0), (0, 0))
+SLIDES = (-2, 0, 2)
+
+
+def met_pixel(d, depth, along, tap):
+    i, j = rim_place(d, depth, along, 2)
+    return i - 2 * tap[0], j - 2 * tap[1]
+
+
+def met_matrix():
+    out = np.zeros((2, LAYER_ROWS, PX), np.float32)
+    for depth in range(2):
+        for row, d, along in layer_rows(2):
+            i, j = met_pixel(d, depth, along, CORNER_TAP[d // 2] if d % 2 else SIDE_TAP[d // 2])
+            out[depth, row, i * SIDE + j] = 1
+    return out.reshape(2 * LAYER_ROWS, PX)
+
+
+def slide_tap(j, slide):
+    target = met_pixel(2 * j, 0, 7 + slide, SIDE_TAP[j])
+    return [(a, b) for a in range(3) for b in range(3) if met_pixel(2 * j, 0, 7, (a, b)) == target][0]
+
+
 def constants():
     pick = np.concatenate([pick_matrix(0), pick_matrix(1)])
     arrays = (
@@ -111,7 +143,7 @@
         rim_matrix(1),
         rim_matrix(2),
         taps_matrix(1),
-        taps_matrix(2),
+        met_matrix(),
     )
     return [jnp.asarray(a, BF16) for a in arrays]
 
@@ -129,12 +161,14 @@
 
 
 def block_kernel(
-    feat, cot, k1, k2, nb, turns,
-    pick, spread, shift1, shift2, rim1, rim2, taps1, taps2,
-    out, fgrad, g1_out, g2_out,
+    feat_in, cot_in, k1_in, k2_in, nb_in, turns_in,
+    pick_in, spread_in, shift1_in, shift2_in, rim1_in, rim2_in, taps1_in, met_in,
+    out_hbm, fgrad_hbm, halves_hbm,
+    feat, cot, k1, k2, nb, turns, pick, spread, shift1, shift2, rim1, rim2, taps1, met,
     buf, msg, recv, choose, kt1, kt2, x1f, x1g, x2h, x2c, zcat, center, mid, deriv,
-    grads, core_in, part, rs_in, z_in, ag_in, sib_in,
-    send_sem, recv_sem, ar_send, ar_recv,
+    strip, strip_in, slid, met_side, met_corner, tap_kernels,
+    grads, core_in, part, rs_in, line_in, ag_in, out, fgrad,
+    send_sem, recv_sem, ar_send, ar_recv, load_sem, store_sem, strip_sem, go_sem,
 ):
     me = lax.axis_index("tile")
     core = me & 1
@@ -143,24 +177,34 @@
     def along(axis, i):
         return me + (((pos[axis] + i) & 3) - pos[axis]) * STRIDE[axis]
 
-    def plane_peers():
-        for dy in range(4):
-            for dx in range(4):
-                if dy or dx:
-                    y, x = (pos["y"] + dy) & 3, (pos["x"] + dx) & 3
-                    yield me + (y - pos["y"]) * STRIDE["y"] + (x - pos["x"]) * STRIDE["x"], y * 4 + x
+    def plane_peers(a, b):
+        steps = [(da, db) for da in range(4) for db in range(4) if da or db]
+        for da, db in sorted(steps, key=lambda step: -sum(min(d, 4 - d) for d in step)):
+            at_a, at_b = (pos[a] + da) & 3, (pos[b] + db) & 3
+            yield me + (at_a - pos[a]) * STRIDE[a] + (at_b - pos[b]) * STRIDE[b], at_b * 4 + at_a
 
     sibling = me + 1 - 2 * core
 
-    peers = [sibling] + [device for device, _ in plane_peers()]
-    for axis in "yxz":
-        for i in range(1, 4):
-            if axis == "z":
-                peers.append(along(axis, i))
-            peers.append(along(axis, i) + 1 - 2 * core)
+    peers = [sibling] + [along(axis, i) for axis in "xyz" for i in FAR_FIRST]
     barrier = pltpu.get_barrier_semaphore()
     for device in peers:
         pl.semaphore_signal(barrier, inc=1, device_id=(device,), device_id_type=MESH)
+
+    loads = {}
+    for i, (name, src, dst) in enumerate(
+        (
+            ("pick", pick_in, pick), ("feat", feat_in, feat), ("met", met_in, met), ("cot", cot_in, cot),
+            ("k2", k2_in, k2), ("nb", nb_in, nb), ("turns", turns_in, turns),
+            ("shift1", shift1_in, shift1), ("shift2", shift2_in, shift2), ("rim1", rim1_in, rim1),
+            ("k1", k1_in, k1), ("spread", spread_in, spread), ("taps1", taps1_in, taps1), ("rim2", rim2_in, rim2),
+        )
+    ):
+        loads[name] = pltpu.make_async_copy(src, dst, load_sem.at[i])
+        loads[name].start()
+
+    def loaded(*names):
+        for name in names:
+            loads[name].wait()
 
     def remote(src, dst, send, arrive, device):
         pltpu.make_async_remote_copy(
@@ -175,28 +219,39 @@
         return pl.ds(pl.multiple_of((pos[b] * 4 + pos[a]) * 16, 16), 16)
 
     def put(layer, values):
-        buf[layer, :, own_rows(layer), :] = values.astype(BF16).reshape(5, 16, CH)
+        n = SLICES[layer]
+        buf[layer, 0:n, own_rows(layer), :] = values[0 : n * 16].astype(BF16).reshape(n, 16, CH)
+
+    def blocks(layer, count):
+        return buf.at[layer, pl.ds(0, SLICES[layer]), pl.ds(0, count * 16), :]
 
     def send_a(layer):
         axis = PLANS[LAYER_PLAN[layer]][0]
-        view = buf.at[layer, :, own_rows(layer), :]
-        for i in range(1, 4):
+        view = buf.at[layer, pl.ds(0, SLICES[layer]), own_rows(layer), :]
+        for i in FAR_FIRST:
             remote(view, view, send_sem.at[layer, 0], recv_sem.at[layer, 0], along(axis, i))
+
+    def gathered(layer):
+        wait_bytes(blocks(layer, 12), recv_sem.at[layer, 1])
 
     def send_b(layer):
         axis = PLANS[LAYER_PLAN[layer]][1]
-        wait_bytes(buf.at[layer, :, pl.ds(0, 48), :], recv_sem.at[layer, 0])
-        view = buf.at[layer, :, pl.ds(pl.multiple_of(pos[axis] * 64, 64), 64), :]
-        for i in range(1, 4):
+        wait_bytes(blocks(layer, 3), recv_sem.at[layer, 0])
+        view = buf.at[layer, pl.ds(0, SLICES[layer]), pl.ds(pl.multiple_of(pos[axis] * 64, 64), 64), :]
+        for i in FAR_FIRST:
             remote(view, view, send_sem.at[layer, 1], recv_sem.at[layer, 1], along(axis, i))
 
     def send_line(layer, chooser):
+        gathered(layer)
+        for q in range(5):
+            source = buf[layer, q if q < 4 else CORNER_SLICE[layer]]
+            msg[layer, q] = dot(choose[chooser, 0 if q < 4 else 1], source).astype(BF16)
+        deliver(layer)
+
+    def deliver(layer):
         axis = PLANS[LAYER_PLAN[layer]][2]
-        wait_bytes(buf.at[layer, :, pl.ds(0, 192), :], recv_sem.at[layer, 1])
-        for q in range(5):
-            msg[layer, q] = dot(choose[chooser, 0 if q < 4 else 1], buf[layer, q]).astype(BF16)
         mine = pl.ds(pl.multiple_of((pos[axis] * 2 + core) * 16, 16), 16)
-        for i in range(4):
+        for i in FAR_FIRST + (0,):
             for flip in range(2):
                 if i or flip:
                     other = core + flip - 2 * core * flip
@@ -208,6 +263,73 @@
                     )
         recv[layer, :, mine, :] = msg[layer, :, mine, :]
 
+    def send_strip(depth, values):
+        axis = PLANS[LAYER_PLAN[1 + depth]][2]
+        strip[depth] = values.astype(BF16).reshape(5, 16, CH)
+        mine = pl.ds(pl.multiple_of((pos[axis] * 2 + core) * 16, 16), 16)
+        for i in FAR_FIRST + (0,):
+            for flip in range(2):
+                if i or flip:
+                    device = along(axis, i) + flip - 2 * core * flip
+                    remote(
+                        strip.at[depth], strip_in.at[depth, :, mine, :],
+                        strip_sem.at[0, depth], strip_sem.at[1, depth], device,
+                    )
+        strip_in[depth, :, mine, :] = strip[depth]
+
+    def meet(layer):
+        gathered(layer)
+        depth = layer - 1
+        lane = lax.broadcasted_iota(jnp.int32, (128, PX), 1) & 3
+        for corner in range(2):
+            full = choose[layer, corner].astype(F32)
+            split = jnp.concatenate([jnp.where(lane == j, full, 0.0).astype(BF16) for j in range(4)], axis=0)
+            for q in (4,) if corner else range(4):
+                found = dot(split, buf[layer, q if q < 4 else CORNER_SLICE[layer]]).astype(BF16)
+                for j in range(4):
+                    part_j = found[j * 128 : (j + 1) * 128]
+                    if corner:
+                        met_corner[depth * 128 : (depth + 1) * 128, j * CH : (j + 1) * CH] = part_j
+                    else:
+                        at = (depth * 4 + q) * 128
+                        met_side[at : at + 128, j * CH : (j + 1) * CH] = part_j
+
+    def slide(x, step):
+        x = x.reshape(4, 8, 2, 8, CH)
+        empty = jnp.zeros((1, 8, 1, 8, CH), F32)
+        first, second = x[:, :, 0:1], x[:, :, 1:2]
+        if step < 0:
+            x = jnp.concatenate([jnp.concatenate([empty, second[0:3]], axis=0), first], axis=2)
+        elif step > 0:
+            x = jnp.concatenate([second, jnp.concatenate([first[1:4], empty], axis=0)], axis=2)
+        return x.reshape(512, CH)
+
+    def send_rim_gradient(layer):
+        depth = layer - 1
+        meet(layer)
+        terms = dot(met_side[depth * 512 : (depth + 1) * 512, :], tap_kernels[:, 0 : 3 * CH])
+        total = None
+        for k, step in enumerate(SLIDES):
+            term = slide(terms[:, k * CH : (k + 1) * CH], step)
+            total = term if total is None else total + term
+        msg[layer, 0:4] = total.astype(BF16).reshape(4, 128, CH)
+        corner = dot(met_corner[depth * 128 : (depth + 1) * 128, :], tap_kernels[:, 3 * CH : 4 * CH])
+        msg[layer, 4] = corner.astype(BF16)
+        deliver(layer)
+
+    def lay_taps():
+        for j in range(4):
+            taps = [slide_tap(j, step) for step in SLIDES] + [CORNER_TAP[j]]
+            for k, (a, b) in enumerate(taps):
+                at = ((2 - a) * 3 + 2 - b) * CH
+                tap_kernels[j * CH : (j + 1) * CH, k * CH : (k + 1) * CH] = kt2[at : at + CH, :]
+
+    def slide_strips(depth):
+        wait_bytes(strip_in.at[depth, :, pl.ds(0, 112), :], strip_sem.at[1, depth])
+        x = strip_in[depth, 0:4].astype(F32)
+        for k, step in enumerate(SLIDES):
+            slid[depth * 512 : (depth + 1) * 512, k * CH : (k + 1) * CH] = slide(x, -step).astype(BF16)
+
     def arrived(layer):
         wait_bytes(recv.at[layer, :, pl.ds(0, 112), :], recv_sem.at[layer, 2])
         total = recv[layer, :, 0:16, :].astype(F32)
@@ -216,8 +338,8 @@
         return total.reshape(LAYER_ROWS, CH)
 
     def finish_sends(layer):
-        wait_bytes(buf.at[layer, :, pl.ds(0, 48), :], send_sem.at[layer, 0])
-        wait_bytes(buf.at[layer, :, pl.ds(0, 192), :], send_sem.at[layer, 1])
+        wait_bytes(blocks(layer, 3), send_sem.at[layer, 0])
+        wait_bytes(blocks(layer, 12), send_sem.at[layer, 1])
         wait_bytes(recv.at[layer, :, pl.ds(0, 112), :], send_sem.at[layer, 2])
 
     def table_rows(device_of_row, column_of_row):
@@ -227,7 +349,9 @@
         keep = lax.broadcasted_iota(jnp.int32, (rows, 8), 1) == column_of_row
         picked = []
         for table in (nb, turns):
-            values = dot(hot, table[...].astype(F32).astype(BF16))
+            values = lax.dot_general(
+                hot, table[...].astype(F32).astype(BF16), (((1,), (1,)), ((), ())), preferred_element_type=F32
+            )
             values = jnp.sum(jnp.where(keep, values, 0.0), axis=1, keepdims=True)
             picked.append(values.astype(jnp.int32))
         return picked
@@ -241,6 +365,8 @@
             source, quarter = table_rows(dest, 2 * j + corner)
             here = (source >= 0) & (coordinate(source, line) == pos[line]) & ((source & 1) == core)
             place = (coordinate(source, b) * 4 + coordinate(source, a)) * 16 + e * 4 + ((j + 2 + quarter) & 3)
+            if corner:
+                here, place = here & (e < 2), place + 8
             place = jnp.where(here, place, -1)
             lanes = lax.broadcasted_iota(jnp.int32, (128, PX), 1)
             choose[slot, corner] = jnp.where(lanes == place, 1.0, 0.0).astype(BF16)
@@ -288,90 +414,110 @@
             zcat[0:rows, tap * CH : (tap + 1) * CH] = shifted.astype(BF16)
         return dot(zcat[0:rows, :], kernel_t[...])
 
+    def put_rows(which, start, values, add=False):
+        at = 0
+        while at < values.shape[0]:
+            i, row = divmod(start + at, CHUNK)
+            size = min(CHUNK - row, values.shape[0] - at)
+            piece = values[at : at + size]
+            if add:
+                piece = piece + grads[which, i, row : row + size, :]
+            grads[which, i, row : row + size, :] = piece
+            at += size
+
     def kernel_gradient(which, x, right, dilation):
         for a in range(3):
             window = x[a * dilation * SIDE : a * dilation * SIDE + PX, :]
-            grads[which, a * 3 * CH : (a + 1) * 3 * CH, :] = dot_first(window, right)
-
-    half = pl.multiple_of(core * 32, 8)
-    other_half = pl.multiple_of(32 - core * 32, 8)
-    owner = pos["y"] * 4 + pos["x"]
+            put_rows(which, a * 3 * CH, dot_first(window, right))
+
+    half = pl.multiple_of(core * (CHUNK - HALF), 8)
+    other_half = pl.multiple_of((1 - core) * (CHUNK - HALF), 8)
+    owners = [pos[b] * 4 + pos[a] for a, b, _ in SUM_PLANS]
 
     def ar_core(which):
-        for i in range(16):
-            remote(
-                grads.at[which, pl.ds(pl.multiple_of(i * 72 + other_half, 8), 40), :], core_in.at[which, i],
-                ar_send.at[which, 0], ar_recv.at[which, 0], sibling,
-            )
+        remote(
+            grads.at[which, :, pl.ds(other_half, HALF), :], core_in.at[which],
+            ar_send.at[which, 0], ar_recv.at[which, 0], sibling,
+        )
 
     def ar_scatter(which):
         wait_bytes(core_in.at[which], ar_recv.at[which, 0])
-        for i in range(16):
-            mine = grads[which, pl.ds(pl.multiple_of(i * 72 + half, 8), 40), :]
-            part[which, i] = mine + core_in[which, i]
-        for device, i in plane_peers():
-            remote(part.at[which, i], rs_in.at[which, owner], ar_send.at[which, 1], ar_recv.at[which, 1], device)
-        rs_in[which, owner] = part[which, owner]
+        part[which] = (grads[which, :, pl.ds(half, HALF), :] + core_in[which]).astype(BF16)
+        for device, i in plane_peers(*SUM_PLANS[which][:2]):
+            remote(
+                part.at[which, i], rs_in.at[which, owners[which]],
+                ar_send.at[which, 1], ar_recv.at[which, 1], device,
+            )
+        rs_in[which, owners[which]] = part[which, owners[which]]
 
     def ar_line(which):
+        axis = SUM_PLANS[which][2]
         wait_bytes(rs_in.at[which, pl.ds(0, 15)], ar_recv.at[which, 1])
-        total = rs_in[which, 0]
+        total = rs_in[which, 0].astype(F32)
         for i in range(1, 16):
-            total += rs_in[which, i]
-        z_in[which, pos["z"]] = total
-        for i in range(1, 4):
+            total += rs_in[which, i].astype(F32)
+        line_in[which, pos[axis]] = total
+        for i in FAR_FIRST:
             remote(
-                z_in.at[which, pos["z"]], z_in.at[which, pos["z"]],
-                ar_send.at[which, 2], ar_recv.at[which, 2], along("z", i),
+                line_in.at[which, pos[axis]], line_in.at[which, pos[axis]],
+                ar_send.at[which, 2], ar_recv.at[which, 2], along(axis, i),
             )
 
     def ar_gather(which):
-        wait_bytes(z_in.at[which, pl.ds(0, 3)], ar_recv.at[which, 2])
-        total = ((z_in[which, 0] + z_in[which, 1]) + z_in[which, 2]) + z_in[which, 3]
-        ag_in[which, owner] = total * SCALE
-        for device, _ in plane_peers():
+        wait_bytes(line_in.at[which, pl.ds(0, 3)], ar_recv.at[which, 2])
+        total = ((line_in[which, 0] + line_in[which, 1]) + line_in[which, 2]) + line_in[which, 3]
+        ag_in[which, owners[which]] = (total * SCALE).astype(BF16)
+        for device, _ in plane_peers(*SUM_PLANS[which][:2]):
             remote(
-                ag_in.at[which, owner], ag_in.at[which, owner],
+                ag_in.at[which, owners[which]], ag_in.at[which, owners[which]],
                 ar_send.at[which, 3], ar_recv.at[which, 3], device,
             )
 
     def ar_share(which):
         wait_bytes(ag_in.at[which, pl.ds(0, 15)], ar_recv.at[which, 3])
-        remote(ag_in.at[which], sib_in.at[which], ar_send.at[which, 4], ar_recv.at[which, 4], sibling)
-
-    def ar_finish(which, dest):
-        wait_bytes(sib_in.at[which], ar_recv.at[which, 4])
-        first = core == 0
-        for i in range(16):
-            mine, theirs = ag_in[which, i], sib_in[which, i]
-            dest[i * 72 : i * 72 + 40, :] = jnp.where(first, mine, theirs)
-            dest[i * 72 + 40 : i * 72 + 72, :] = jnp.where(first, theirs, mine)[8:40]
+        remote(ag_in.at[which], halves_hbm.at[which, core], ar_send.at[which, 4], ar_recv.at[which, 4], sibling)
+        pltpu.make_async_copy(ag_in.at[which], halves_hbm.at[which, core], store_sem.at[which]).start()
+
+    def ar_finish(which):
+        wait_bytes(ag_in.at[which], ar_recv.at[which, 4])
+        pltpu.make_async_copy(ag_in.at[which], halves_hbm.at[which, core], store_sem.at[which]).wait()
+
+    def ar_sent(which):
         wait_bytes(core_in.at[which], ar_send.at[which, 0])
         wait_bytes(rs_in.at[which, pl.ds(0, 15)], ar_send.at[which, 1])
-        wait_bytes(z_in.at[which, pl.ds(0, 3)], ar_send.at[which, 2])
+        wait_bytes(line_in.at[which, pl.ds(0, 3)], ar_send.at[which, 2])
         wait_bytes(ag_in.at[which, pl.ds(0, 15)], ar_send.at[which, 3])
-        wait_bytes(sib_in.at[which], ar_send.at[which, 4])
-
+        wait_bytes(ag_in.at[which], ar_send.at[which, 4])
+
+    loaded("pick", "feat")
     put(0, dot(pick[0:LAYER_ROWS, :], feat[...]))
-    flip_kernel(k2, kt2)
-    rim = rim_gradient(cot[...], taps2, kt2, SECOND)
-    put(1, rim[0:LAYER_ROWS])
-    put(2, rim[LAYER_ROWS : 2 * LAYER_ROWS])
+    loaded("met", "cot")
+    rows = dot(met[...], cot[...])
+    put(1, rows[0:LAYER_ROWS])
+    put(2, rows[LAYER_ROWS : 2 * LAYER_ROWS])
     pl.semaphore_wait(barrier, len(peers))
+    pl.semaphore_signal(go_sem, inc=1, device_id=(sibling,), device_id_type=MESH)
     for layer in range(3):
         send_a(layer)
+    loaded("nb", "turns", "shift1", "shift2")
     build_forward(0, 0)
     build_adjoint(1, 1)
     build_adjoint(2, 2)
     for layer in range(3):
         send_b(layer)
+    loaded("k2")
+    flip_kernel(k2, kt2)
+    lay_taps()
     center[0 : 3 * 288, :] = dot(shift1[...], feat[...])
     lay(x2c, dot(shift2[...], cot[...]))
     mid[...] = conv(x2c, lambda a: kt2[a * 384 : (a + 1) * 384, :], SECOND).astype(BF16)
-    for layer in range(3):
-        send_line(layer, layer)
+    loaded("k1", "rim1", "spread", "taps1", "rim2")
     flip_kernel(k1, kt1)
     build_forward(3, 2)
+    pl.semaphore_wait(go_sem, 1)
+    send_line(0, 0)
+    send_rim_gradient(1)
+    send_rim_gradient(2)
 
     lay(x1f, center[0 : 3 * 288, :] + dot(rim1[...], arrived(0).astype(BF16)))
     v = conv(x1f, lambda a: k1[a], FIRST)
@@ -385,6 +531,8 @@
     put(4, rows[LAYER_ROWS : 2 * LAYER_ROWS])
     send_a(3)
     send_a(4)
+    send_strip(0, rows[0:LAYER_ROWS])
+    send_strip(1, rows[LAYER_ROWS : 2 * LAYER_ROWS])
 
     sums = jnp.concatenate([arrived(1), arrived(2)], axis=0)
     high = sums.astype(BF16)
@@ -395,63 +543,118 @@
     send_a(5)
     kernel_gradient(0, x1f, gpre, FIRST)
     ar_core(0)
+
+    center[...] = dot(shift2[...], hidden)
+    lay(x2h, center[...])
+    kernel_gradient(1, x2h, cot[...], SECOND)
     send_b(3)
     send_b(4)
-    center[...] = dot(shift2[...], hidden)
+    ar_scatter(0)
+    slide_strips(0)
+    slide_strips(1)
+    sides = dot_first(slid[...], met_side[...])
+    corners = dot_first(strip_in[:, 4].reshape(256, CH), met_corner[...])
+    for j in range(4):
+        pieces = [(CORNER_TAP[j], corners[:, j * CH : (j + 1) * CH])]
+        for k, slide in enumerate(SLIDES):
+            pieces.append((slide_tap(j, slide), sides[k * CH : (k + 1) * CH, j * CH : (j + 1) * CH]))
+        for (a, b), piece in pieces:
+            put_rows(1, (a * 3 + b) * CH, piece, add=True)
+    ar_core(1)
     send_b(5)
+    ar_scatter(1)
     lay(x1g, dot(shift1[...], gpre))
     mid[...] = conv(x1g, lambda a: kt1[a * 384 : (a + 1) * 384, :], FIRST).astype(BF16)
-    ar_scatter(0)
     send_line(3, 0)
     send_line(4, 3)
+    ar_line(0)
+    ar_line(1)
     send_line(5, 1)
-    ar_line(0)
-
+
+    ar_gather(0)
     rims = jnp.concatenate([arrived(3), arrived(4)], axis=0).astype(BF16)
     lay(x2h, center[...] + dot(rim2[...], rims))
-    kernel_gradient(1, x2h, cot[...], SECOND)
-    ar_core(1)
     out[...] = conv(x2h, lambda a: k2[a], SECOND).astype(BF16)
-    ar_gather(0)
-    ar_scatter(1)
+    stores = [
+        pltpu.make_async_copy(out, out_hbm, store_sem.at[2]),
+        pltpu.make_async_copy(fgrad, fgrad_hbm, store_sem.at[3]),
+    ]
+    stores[0].start()
+    ar_gather(1)
     sums = arrived(5)
     high = sums.astype(BF16)
     low = (sums - high.astype(F32)).astype(BF16)
     fgrad[...] = (
         mid[...].astype(F32) + dot(spread[:, 0:LAYER_ROWS], high) + dot(spread[:, 0:LAYER_ROWS], low)
     ).astype(BF16)
+    stores[1].start()
     ar_share(0)
-    ar_line(1)
-    ar_finish(0, g1_out)
-    ar_gather(1)
-    for layer in range(6):
+    ar_share(1)
+    for layer in range(LAYERS):
         finish_sends(layer)
-    ar_share(1)
-    ar_finish(1, g2_out)
+    for depth in range(2):
+        wait_bytes(strip_in.at[depth, :, pl.ds(0, 112), :], strip_sem.at[0, depth])
+    for copy in stores:
+        copy.wait()
+    for which in range(2):
+        ar_finish(which)
+        ar_sent(which)
+
+
+def store_kernel(out_in, fgrad_in, halves_in, out_to, fgrad_to, first_to, second_to, out, fgrad, halves, grads, sem):
+    def load(i, src, dst):
+        copy = pltpu.make_async_copy(src, dst, sem.at[0, i])
+        copy.start()
+        return copy
+
+    def store(i, src, dst):
+        copy = pltpu.make_async_copy(src, dst, sem.at[1, i])
+        copy.start()
+        return copy
+
+    loads = [
+        load(0, halves_in.at[1], halves.at[1]),
+        load(1, halves_in.at[0], halves.at[0]),
+        load(2, out_in, out),
+        load(3, fgrad_in, fgrad),
+    ]
+    stores = []
+    for k, which in enumerate((1, 0)):
+        loads[k].wait()
+        for i in range(16):
+            at = i * CHUNK
+            grads[which, at : at + HALF, :] = halves[which, 0, i].astype(F32)
+            grads[which, at + HALF : at + CHUNK, :] = halves[which, 1, i].astype(F32)[2 * HALF - CHUNK : HALF]
+        stores.append(store(k, grads.at[which], (first_to, second_to)[which]))
+    loads[2].wait()
+    stores.append(store(2, out, out_to))
+    loads[3].wait()
+    stores.append(store(3, fgrad, fgrad_to))
+    for copy in stores:
+        copy.wait()
 
 
 def local(features, cotangent, kernel_first_layer, kernel_second_layer, neighbors, turns):
-    vmem = pl.BlockSpec(memory_space=pltpu.VMEM)
     operands = [
         features.reshape(PX, CH),
         cotangent.reshape(PX, CH),
         kernel_first_layer.reshape(3, 3 * CH, CH),
         kernel_second_layer.reshape(3, 3 * CH, CH),
-        neighbors,
-        turns,
+        neighbors.T,
+        turns.T,
     ] + constants()
-    output, features_gradient, first, second = pl.pallas_call(
+    hbm = pl.BlockSpec(memory_space=pltpu.HBM)
+    tile = jax.ShapeDtypeStruct((PX, CH), BF16)
+    halves = jax.ShapeDtypeStruct((2, 2, 16, HALF, CH), BF16)
+    grad = jax.ShapeDtypeStruct((9 * CH, CH), F32)
+    results = pl.pallas_call(
         block_kernel,
-        out_shape=(
-            jax.ShapeDtypeStruct((PX, CH), BF16),
-            jax.ShapeDtypeStruct((PX, CH), BF16),
-            jax.ShapeDtypeStruct((9 * CH, CH), F32),
-            jax.ShapeDtypeStruct((9 * CH, CH), F32),
-        ),
-        in_specs=[vmem] * len(operands),
-        out_specs=(vmem,) * 4,
-        scratch_shapes=[
-            pltpu.VMEM((6, 5, 256, CH), BF16),
+        out_shape=(tile, tile, halves),
+        in_specs=[hbm] * len(operands),
+        out_specs=(hbm,) * 3,
+        scratch_shapes=[pltpu.VMEM(x.shape, x.dtype) for x in operands]
+        + [
+            pltpu.VMEM((LAYERS, 5, 256, CH), BF16),
             pltpu.VMEM((6, 5, 128, CH), BF16),
             pltpu.VMEM((6, 5, 128, CH), BF16),
             pltpu.VMEM((4, 2, 128, PX), BF16),
@@ -461,26 +664,51 @@
             pltpu.VMEM((288, 3 * CH), BF16),
             pltpu.VMEM((320, 3 * CH), BF16),
             pltpu.VMEM((320, 3 * CH), BF16),
-            pltpu.VMEM((2 * LAYER_ROWS, 9 * CH), BF16),
+            pltpu.VMEM((LAYER_ROWS, 9 * CH), BF16),
             pltpu.VMEM((3 * 320, CH), F32),
             pltpu.VMEM((PX, CH), BF16),
             pltpu.VMEM((PX, CH), F32),
-            pltpu.VMEM((2, 9 * CH, CH), F32),
-            pltpu.VMEM((2, 16, 40, CH), F32),
-            pltpu.VMEM((2, 16, 40, CH), F32),
-            pltpu.VMEM((2, 16, 40, CH), F32),
-            pltpu.VMEM((2, 4, 40, CH), F32),
-            pltpu.VMEM((2, 16, 40, CH), F32),
-            pltpu.VMEM((2, 16, 40, CH), F32),
-            pltpu.SemaphoreType.DMA((6, 3)),
-            pltpu.SemaphoreType.DMA((6, 3)),
+            pltpu.VMEM((2, 5, 16, CH), BF16),
+            pltpu.VMEM((2, 5, 128, CH), BF16),
+            pltpu.VMEM((1024, 3 * CH), BF16),
+            pltpu.VMEM((1024, 4 * CH), BF16),
+            pltpu.VMEM((256, 4 * CH), BF16),
+            pltpu.VMEM((4 * CH, 4 * CH), BF16),
+            pltpu.VMEM((2, 16, CHUNK, CH), F32),
+            pltpu.VMEM((2, 16, HALF, CH), F32),
+            pltpu.VMEM((2, 16, HALF, CH), BF16),
+            pltpu.VMEM((2, 16, HALF, CH), BF16),
+            pltpu.VMEM((2, 4, HALF, CH), F32),
+            pltpu.VMEM((2, 16, HALF, CH), BF16),
+            pltpu.VMEM((PX, CH), BF16),
+            pltpu.VMEM((PX, CH), BF16),
+            pltpu.SemaphoreType.DMA((LAYERS, 3)),
+            pltpu.SemaphoreType.DMA((LAYERS, 3)),
             pltpu.SemaphoreType.DMA((2, 5)),
             pltpu.SemaphoreType.DMA((2, 5)),
+            pltpu.SemaphoreType.DMA((len(operands),)),
+            pltpu.SemaphoreType.DMA((4,)),
+            pltpu.SemaphoreType.DMA((2, 2)),
+            pltpu.SemaphoreType.REGULAR,
         ],
         compiler_params=pltpu.CompilerParams(
-            collective_id=0, has_side_effects=True, vmem_limit_bytes=48 * 2**20
+            collective_id=0, has_side_effects=True, vmem_limit_bytes=60 * 2**20
         ),
     )(*operands)
+    output, features_gradient, first, second = pl.pallas_call(
+        store_kernel,
+        out_shape=(tile, tile, grad, grad),
+        in_specs=[hbm] * 3,
+        out_specs=(hbm,) * 4,
+        scratch_shapes=[
+            pltpu.VMEM((PX, CH), BF16),
+            pltpu.VMEM((PX, CH), BF16),
+            pltpu.VMEM((2, 2, 16, HALF, CH), BF16),
+            pltpu.VMEM((2, 9 * CH, CH), F32),
+            pltpu.SemaphoreType.DMA((2, 4)),
+        ],
+        compiler_params=pltpu.CompilerParams(vmem_limit_bytes=60 * 2**20),
+    )(*results)
     return (
         output.reshape(features.shape),
         features_gradient.reshape(features.shape),

time: 78 us -> 48.7 us (0.62)
  local copies, waits for them, and re-layouts: 15.1 us -> 0 us
  Pallas kernels: 61.6 us -> 47.9 us
    unnamed x30 -> x0, local copies, waits for them, and re-layouts: 15.1 us -> none
    pallas_call x1 -> x2, Pallas kernels: 61.6 us -> 47.9 us  [the longest x1 45.7 us: local(): pl.pallas_call(block_kernel, out_shape=(tile, tile, halves), in_specs=[hb...]
where the time goes in v2:
time: 48.7 us; the launch traced here: 48.5 us
  Pallas kernels  47.9 us (98%)
  between operations  0.64 us (1%)
    pallas_call x1, Pallas kernels, local(): pl.pallas_call(block_kernel, out_shape=(tile, tile, halves), in_specs=[hb...  45.7 us
    pallas_call x1, Pallas kernels, local(): pl.pallas_call(store_kernel, out_shape=(tile, tile, grad, grad), in_specs...  2.14 us

profile of v2, /device:TPU:1, one launch (start us, length us, event | category | flops | bytes accessed | tf_op | source)
XLA Modules:
  0.0 48.5 jit_solution(18039581376567197048)
XLA Ops:
  0.6 45.7 %shard_map.165 = (bf16[256,128]{1,0:T(8,128)(2,1)}, bf16[256,128]{1,0:T(8,128)(2,1)}, bf16[2,2,16,48,128]{4,3,2,1,0:T(8,128)(2,1)}) custom-call(bf16[256,128]{1,0:T(8,128)(2,1)} %bitcast.12, bf16[256,128]{1,0:T(8,128)(2,1)} %bitcast.13, bf16[3,384,128]{2,1,0:T(8,128)(2,1)} %bitcast.10, bf16[3,384,128]{2,1,0:T(8,128)(2,1)} %bitcast.11, s32[8,128]{1,0:T(8,128)} %bitcast.14, ...), custom_call_target="tpu_custom_call" | custom-call | tf_op jit(solution)/shard_map/pallas_call | solution.py:650
  46.4 2.1 %shard_map.166 = (bf16[256,128]{1,0:T(8,128)(2,1)}, bf16[256,128]{1,0:T(8,128)(2,1)}, f32[1152,128]{1,0:T(8,128)}, f32[1152,128]{1,0:T(8,128)}) custom-call(bf16[256,128]{1,0:T(8,128)(2,1)} %get-tuple-element.11.out_in, bf16[256,128]{1,0:T(8,128)(2,1)} %get-tuple-element.12.fgrad_in, bf16[2,2,16,48,128]{4,3,2,1,0:T(8,128)(2,1)} %get-tuple-element.13.halves_in), custom_call_target="tpu_custom_call" | custom-call | tf_op jit(solution)/shard_map/pallas_call | solution.py:698

commit v3 on v2

--- a/solution.py
+++ b/solution.py
@@ -37,7 +37,7 @@
 
 FAR_FIRST = (2, 1, 3)
 
-CHUNK, HALF = 72, 48
+CHUNK, SENT = 72, 80
 SUM_PLANS = (("z", "x", "y"), ("x", "y", "z"))
 
 
@@ -163,7 +163,7 @@
 def block_kernel(
     feat_in, cot_in, k1_in, k2_in, nb_in, turns_in,
     pick_in, spread_in, shift1_in, shift2_in, rim1_in, rim2_in, taps1_in, met_in,
-    out_hbm, fgrad_hbm, halves_hbm,
+    out_hbm, fgrad_hbm, sums_hbm,
     feat, cot, k1, k2, nb, turns, pick, spread, shift1, shift2, rim1, rim2, taps1, met,
     buf, msg, recv, choose, kt1, kt2, x1f, x1g, x2h, x2c, zcat, center, mid, deriv,
     strip, strip_in, slid, met_side, met_corner, tap_kernels,
@@ -177,7 +177,8 @@
     def along(axis, i):
         return me + (((pos[axis] + i) & 3) - pos[axis]) * STRIDE[axis]
 
-    def plane_peers(a, b):
+    def plane_peers(which):
+        a, b, _ = SUM_PLANS[which]
         steps = [(da, db) for da in range(4) for db in range(4) if da or db]
         for da, db in sorted(steps, key=lambda step: -sum(min(d, 4 - d) for d in step)):
             at_a, at_b = (pos[a] + da) & 3, (pos[b] + db) & 3
@@ -430,64 +431,65 @@
             window = x[a * dilation * SIDE : a * dilation * SIDE + PX, :]
             put_rows(which, a * 3 * CH, dot_first(window, right))
 
-    half = pl.multiple_of(core * (CHUNK - HALF), 8)
-    other_half = pl.multiple_of((1 - core) * (CHUNK - HALF), 8)
     owners = [pos[b] * 4 + pos[a] for a, b, _ in SUM_PLANS]
 
+    def padded(chunk):
+        return jnp.concatenate([chunk, jnp.zeros(chunk.shape[:-2] + (SENT - CHUNK, CH), F32)], axis=-2).astype(BF16)
+
     def ar_core(which):
-        remote(
-            grads.at[which, :, pl.ds(other_half, HALF), :], core_in.at[which],
-            ar_send.at[which, 0], ar_recv.at[which, 0], sibling,
-        )
+        @pl.when(core != which)
+        def _():
+            remote(grads.at[which], core_in, ar_send.at[0], ar_recv.at[0], sibling)
 
     def ar_scatter(which):
-        wait_bytes(core_in.at[which], ar_recv.at[which, 0])
-        part[which] = (grads[which, :, pl.ds(half, HALF), :] + core_in[which]).astype(BF16)
-        for device, i in plane_peers(*SUM_PLANS[which][:2]):
-            remote(
-                part.at[which, i], rs_in.at[which, owners[which]],
-                ar_send.at[which, 1], ar_recv.at[which, 1], device,
-            )
-        rs_in[which, owners[which]] = part[which, owners[which]]
+        @pl.when(core == which)
+        def _():
+            wait_bytes(core_in, ar_recv.at[0])
+            for i in range(16):
+                part[i] = padded(grads[which, i] + core_in[i])
+            for device, i in plane_peers(which):
+                remote(part.at[i], rs_in.at[owners[which]], ar_send.at[1], ar_recv.at[1], device)
+            rs_in[owners[which]] = part[owners[which]]
 
     def ar_line(which):
         axis = SUM_PLANS[which][2]
-        wait_bytes(rs_in.at[which, pl.ds(0, 15)], ar_recv.at[which, 1])
-        total = rs_in[which, 0].astype(F32)
-        for i in range(1, 16):
-            total += rs_in[which, i].astype(F32)
-        line_in[which, pos[axis]] = total
-        for i in FAR_FIRST:
-            remote(
-                line_in.at[which, pos[axis]], line_in.at[which, pos[axis]],
-                ar_send.at[which, 2], ar_recv.at[which, 2], along(axis, i),
-            )
+
+        @pl.when(core == which)
+        def _():
+            wait_bytes(rs_in.at[pl.ds(0, 15)], ar_recv.at[1])
+            total = rs_in[0].astype(F32)
+            for i in range(1, 16):
+                total += rs_in[i].astype(F32)
+            line_in[pos[axis]] = total[0:CHUNK]
+            for i in FAR_FIRST:
+                view = line_in.at[pos[axis]]
+                remote(view, view, ar_send.at[2], ar_recv.at[2], along(axis, i))
 
     def ar_gather(which):
-        wait_bytes(line_in.at[which, pl.ds(0, 3)], ar_recv.at[which, 2])
-        total = ((line_in[which, 0] + line_in[which, 1]) + line_in[which, 2]) + line_in[which, 3]
-        ag_in[which, owners[which]] = (total * SCALE).astype(BF16)
-        for device, _ in plane_peers(*SUM_PLANS[which][:2]):
-            remote(
-                ag_in.at[which, owners[which]], ag_in.at[which, owners[which]],
-                ar_send.at[which, 3], ar_recv.at[which, 3], device,
-            )
+        @pl.when(core == which)
+        def _():
+            wait_bytes(line_in.at[pl.ds(0, 3)], ar_recv.at[2])
+            total = ((line_in[0] + line_in[1]) + line_in[2]) + line_in[3]
+            ag_in[owners[which]] = padded(total * SCALE)
+            for device, _ in plane_peers(which):
+                view = ag_in.at[owners[which]]
+                remote(view, view, ar_send.at[3], ar_recv.at[3], device)
 
     def ar_share(which):
-        wait_bytes(ag_in.at[which, pl.ds(0, 15)], ar_recv.at[which, 3])
-        remote(ag_in.at[which], halves_hbm.at[which, core], ar_send.at[which, 4], ar_recv.at[which, 4], sibling)
-        pltpu.make_async_copy(ag_in.at[which], halves_hbm.at[which, core], store_sem.at[which]).start()
-
-    def ar_finish(which):
-        wait_bytes(ag_in.at[which], ar_recv.at[which, 4])
-        pltpu.make_async_copy(ag_in.at[which], halves_hbm.at[which, core], store_sem.at[which]).wait()
-
-    def ar_sent(which):
-        wait_bytes(core_in.at[which], ar_send.at[which, 0])
-        wait_bytes(rs_in.at[which, pl.ds(0, 15)], ar_send.at[which, 1])
-        wait_bytes(line_in.at[which, pl.ds(0, 3)], ar_send.at[which, 2])
-        wait_bytes(ag_in.at[which, pl.ds(0, 15)], ar_send.at[which, 3])
-        wait_bytes(ag_in.at[which], ar_send.at[which, 4])
+        @pl.when(core == which)
+        def _():
+            wait_bytes(ag_in.at[pl.ds(0, 15)], ar_recv.at[3])
+            remote(ag_in, sums_hbm.at[which], ar_send.at[4], ar_recv.at[4], sibling)
+            pltpu.make_async_copy(ag_in, sums_hbm.at[which], store_sem.at[0]).start()
+
+    def ar_finish():
+        wait_bytes(ag_in, ar_recv.at[4])
+        wait_bytes(ag_in, store_sem.at[0])
+        wait_bytes(core_in, ar_send.at[0])
+        wait_bytes(rs_in.at[pl.ds(0, 15)], ar_send.at[1])
+        wait_bytes(line_in.at[pl.ds(0, 3)], ar_send.at[2])
+        wait_bytes(ag_in.at[pl.ds(0, 15)], ar_send.at[3])
+        wait_bytes(ag_in, ar_send.at[4])
 
     loaded("pick", "feat")
     put(0, dot(pick[0:LAYER_ROWS, :], feat[...]))
@@ -596,12 +598,10 @@
         wait_bytes(strip_in.at[depth, :, pl.ds(0, 112), :], strip_sem.at[0, depth])
     for copy in stores:
         copy.wait()
-    for which in range(2):
-        ar_finish(which)
-        ar_sent(which)
-
-
-def store_kernel(out_in, fgrad_in, halves_in, out_to, fgrad_to, first_to, second_to, out, fgrad, halves, grads, sem):
+    ar_finish()
+
+
+def store_kernel(out_in, fgrad_in, sums_from, out_to, fgrad_to, first_to, second_to, out, fgrad, sums_in, grads, sem):
     def load(i, src, dst):
         copy = pltpu.make_async_copy(src, dst, sem.at[0, i])
         copy.start()
@@ -613,8 +613,8 @@
         return copy
 
     loads = [
-        load(0, halves_in.at[1], halves.at[1]),
-        load(1, halves_in.at[0], halves.at[0]),
+        load(0, sums_from.at[1], sums_in.at[1]),
+        load(1, sums_from.at[0], sums_in.at[0]),
         load(2, out_in, out),
         load(3, fgrad_in, fgrad),
     ]
@@ -623,8 +623,7 @@
         loads[k].wait()
         for i in range(16):
             at = i * CHUNK
-            grads[which, at : at + HALF, :] = halves[which, 0, i].astype(F32)
-            grads[which, at + HALF : at + CHUNK, :] = halves[which, 1, i].astype(F32)[2 * HALF - CHUNK : HALF]
+            grads[which, at : at + CHUNK, :] = sums_in[which, i].astype(F32)[0:CHUNK]
         stores.append(store(k, grads.at[which], (first_to, second_to)[which]))
     loads[2].wait()
     stores.append(store(2, out, out_to))
@@ -645,11 +644,11 @@
     ] + constants()
     hbm = pl.BlockSpec(memory_space=pltpu.HBM)
     tile = jax.ShapeDtypeStruct((PX, CH), BF16)
-    halves = jax.ShapeDtypeStruct((2, 2, 16, HALF, CH), BF16)
+    sums_in = jax.ShapeDtypeStruct((2, 16, SENT, CH), BF16)
     grad = jax.ShapeDtypeStruct((9 * CH, CH), F32)
     results = pl.pallas_call(
         block_kernel,
-        out_shape=(tile, tile, halves),
+        out_shape=(tile, tile, sums_in),
         in_specs=[hbm] * len(operands),
         out_specs=(hbm,) * 3,
         scratch_shapes=[pltpu.VMEM(x.shape, x.dtype) for x in operands]
@@ -675,17 +674,17 @@
             pltpu.VMEM((256, 4 * CH), BF16),
             pltpu.VMEM((4 * CH, 4 * CH), BF16),
             pltpu.VMEM((2, 16, CHUNK, CH), F32),
-            pltpu.VMEM((2, 16, HALF, CH), F32),
-            pltpu.VMEM((2, 16, HALF, CH), BF16),
-            pltpu.VMEM((2, 16, HALF, CH), BF16),
-            pltpu.VMEM((2, 4, HALF, CH), F32),
-            pltpu.VMEM((2, 16, HALF, CH), BF16),
+            pltpu.VMEM((16, CHUNK, CH), F32),
+            pltpu.VMEM((16, SENT, CH), BF16),
+            pltpu.VMEM((16, SENT, CH), BF16),
+            pltpu.VMEM((4, CHUNK, CH), F32),
+            pltpu.VMEM((16, SENT, CH), BF16),
             pltpu.VMEM((PX, CH), BF16),
             pltpu.VMEM((PX, CH), BF16),
             pltpu.SemaphoreType.DMA((LAYERS, 3)),
             pltpu.SemaphoreType.DMA((LAYERS, 3)),
-            pltpu.SemaphoreType.DMA((2, 5)),
-            pltpu.SemaphoreType.DMA((2, 5)),
+            pltpu.SemaphoreType.DMA((5,)),
+            pltpu.SemaphoreType.DMA((5,)),
             pltpu.SemaphoreType.DMA((len(operands),)),
             pltpu.SemaphoreType.DMA((4,)),
             pltpu.SemaphoreType.DMA((2, 2)),
@@ -703,7 +702,7 @@
         scratch_shapes=[
             pltpu.VMEM((PX, CH), BF16),
             pltpu.VMEM((PX, CH), BF16),
-            pltpu.VMEM((2, 2, 16, HALF, CH), BF16),
+            pltpu.VMEM((2, 16, SENT, CH), BF16),
             pltpu.VMEM((2, 9 * CH, CH), F32),
             pltpu.SemaphoreType.DMA((2, 4)),
         ],

time: 48.7 us -> 47.8 us (0.982)
  Pallas kernels: 47.9 us -> 47 us
    pallas_call x1, Pallas kernels: 45.7 us -> 44.8 us  [local(): pl.pallas_call(block_kernel, out_shape=(tile, tile, sums_in), in_specs=[h...]
where the time goes in v3:
time: 47.8 us; the launch traced here: 47.6 us
  Pallas kernels  47 us (98%)
  between operations  0.64 us (1%)
    pallas_call x1, Pallas kernels, local(): pl.pallas_call(block_kernel, out_shape=(tile, tile, sums_in), in_specs=[h...  44.8 us
    pallas_call x1, Pallas kernels, local(): pl.pallas_call(store_kernel, out_shape=(tile, tile, grad, grad), in_specs...  2.12 us

profile of v3, /device:TPU:1, one launch (start us, length us, event | category | flops | bytes accessed | tf_op | source)
XLA Modules:
  0.0 47.6 jit_solution(13224680311517466076)
XLA Ops:
  0.6 44.8 %shard_map.165 = (bf16[256,128]{1,0:T(8,128)(2,1)}, bf16[256,128]{1,0:T(8,128)(2,1)}, bf16[2,16,80,128]{3,2,1,0:T(8,128)(2,1)}) custom-call(bf16[256,128]{1,0:T(8,128)(2,1)} %bitcast.12, bf16[256,128]{1,0:T(8,128)(2,1)} %bitcast.13, bf16[3,384,128]{2,1,0:T(8,128)(2,1)} %bitcast.10, bf16[3,384,128]{2,1,0:T(8,128)(2,1)} %bitcast.11, s32[8,128]{1,0:T(8,128)} %bitcast.14, ...), custom_call_target="tpu_custom_call" | custom-call | tf_op jit(solution)/shard_map/pallas_call | solution.py:649
  45.5 2.1 %shard_map.166 = (bf16[256,128]{1,0:T(8,128)(2,1)}, bf16[256,128]{1,0:T(8,128)(2,1)}, f32[1152,128]{1,0:T(8,128)}, f32[1152,128]{1,0:T(8,128)}) custom-call(bf16[256,128]{1,0:T(8,128)(2,1)} %get-tuple-element.11.out_in, bf16[256,128]{1,0:T(8,128)(2,1)} %get-tuple-element.12.fgrad_in, bf16[2,16,80,128]{3,2,1,0:T(8,128)(2,1)} %get-tuple-element.13.sums_from), custom_call_target="tpu_custom_call" | custom-call | tf_op jit(solution)/shard_map/pallas_call | solution.py:697

commit v4 on v3

--- a/solution.py
+++ b/solution.py
@@ -536,19 +536,19 @@
     send_strip(0, rows[0:LAYER_ROWS])
     send_strip(1, rows[LAYER_ROWS : 2 * LAYER_ROWS])
 
+    center[...] = dot(shift2[...], hidden)
+    lay(x2h, center[...])
+    kernel_gradient(1, x2h, cot[...], SECOND)
     sums = jnp.concatenate([arrived(1), arrived(2)], axis=0)
     high = sums.astype(BF16)
     low = (sums - high.astype(F32)).astype(BF16)
     grad_hidden = mid[...].astype(F32) + dot(spread[...], high) + dot(spread[...], low)
     gpre = (grad_hidden * deriv[...]).astype(BF16)
+    kernel_gradient(0, x1f, gpre, FIRST)
+    ar_core(0)
     put(5, rim_gradient(gpre, taps1, kt1, FIRST))
     send_a(5)
-    kernel_gradient(0, x1f, gpre, FIRST)
-    ar_core(0)
-
-    center[...] = dot(shift2[...], hidden)
-    lay(x2h, center[...])
-    kernel_gradient(1, x2h, cot[...], SECOND)
+
     send_b(3)
     send_b(4)
     ar_scatter(0)
@@ -568,8 +568,8 @@
     lay(x1g, dot(shift1[...], gpre))
     mid[...] = conv(x1g, lambda a: kt1[a * 384 : (a + 1) * 384, :], FIRST).astype(BF16)
     send_line(3, 0)
+    ar_line(0)
     send_line(4, 3)
-    ar_line(0)
     ar_line(1)
     send_line(5, 1)
 

time: 47.8 us -> 47.8 us (level)
  no operation moved by 1% of the time
where the time goes in v4:
time: 47.8 us; the launch traced here: 47.7 us
  Pallas kernels  47.1 us (99%)
  between operations  0.64 us (1%)
    pallas_call x1, Pallas kernels, local(): pl.pallas_call(block_kernel, out_shape=(tile, tile, sums_in), in_specs=[h...  44.9 us
    pallas_call x1, Pallas kernels, local(): pl.pallas_call(store_kernel, out_shape=(tile, tile, grad, grad), in_specs...  2.12 us

profile of v4, /device:TPU:1, one launch (start us, length us, event | category | flops | bytes accessed | tf_op | source)
XLA Modules:
  0.0 47.7 jit_solution(14389156161875592870)
XLA Ops:
  0.6 44.9 %shard_map.165 = (bf16[256,128]{1,0:T(8,128)(2,1)}, bf16[256,128]{1,0:T(8,128)(2,1)}, bf16[2,16,80,128]{3,2,1,0:T(8,128)(2,1)}) custom-call(bf16[256,128]{1,0:T(8,128)(2,1)} %bitcast.12, bf16[256,128]{1,0:T(8,128)(2,1)} %bitcast.13, bf16[3,384,128]{2,1,0:T(8,128)(2,1)} %bitcast.10, bf16[3,384,128]{2,1,0:T(8,128)(2,1)} %bitcast.11, s32[8,128]{1,0:T(8,128)} %bitcast.14, ...), custom_call_target="tpu_custom_call" | custom-call | tf_op jit(solution)/shard_map/pallas_call | solution.py:649
  45.6 2.1 %shard_map.166 = (bf16[256,128]{1,0:T(8,128)(2,1)}, bf16[256,128]{1,0:T(8,128)(2,1)}, f32[1152,128]{1,0:T(8,128)}, f32[1152,128]{1,0:T(8,128)}) custom-call(bf16[256,128]{1,0:T(8,128)(2,1)} %get-tuple-element.11.out_in, bf16[256,128]{1,0:T(8,128)(2,1)} %get-tuple-element.12.fgrad_in, bf16[2,16,80,128]{3,2,1,0:T(8,128)(2,1)} %get-tuple-element.13.sums_from), custom_call_target="tpu_custom_call" | custom-call | tf_op jit(solution)/shard_map/pallas_call | solution.py:697

commit v5 on v4

--- a/solution.py
+++ b/solution.py
@@ -574,6 +574,7 @@
     send_line(5, 1)
 
     ar_gather(0)
+    ar_gather(1)
     rims = jnp.concatenate([arrived(3), arrived(4)], axis=0).astype(BF16)
     lay(x2h, center[...] + dot(rim2[...], rims))
     out[...] = conv(x2h, lambda a: k2[a], SECOND).astype(BF16)
@@ -582,7 +583,6 @@
         pltpu.make_async_copy(fgrad, fgrad_hbm, store_sem.at[3]),
     ]
     stores[0].start()
-    ar_gather(1)
     sums = arrived(5)
     high = sums.astype(BF16)
     low = (sums - high.astype(F32)).astype(BF16)

time: 47.8 us -> 47.7 us (level)
  no operation moved by 1% of the time
where the time goes in v5:
time: 47.7 us; the launch traced here: 47.6 us
  Pallas kernels  46.9 us (98%)
  between operations  0.64 us (1%)
    pallas_call x1, Pallas kernels, local(): pl.pallas_call(block_kernel, out_shape=(tile, tile, sums_in), in_specs=[h...  44.8 us
    pallas_call x1, Pallas kernels, local(): pl.pallas_call(store_kernel, out_shape=(tile, tile, grad, grad), in_specs...  2.12 us

profile of v5, /device:TPU:1, one launch (start us, length us, event | category | flops | bytes accessed | tf_op | source)
XLA Modules:
  0.0 47.6 jit_solution(12559594419474484572)
XLA Ops:
  0.6 44.8 %shard_map.165 = (bf16[256,128]{1,0:T(8,128)(2,1)}, bf16[256,128]{1,0:T(8,128)(2,1)}, bf16[2,16,80,128]{3,2,1,0:T(8,128)(2,1)}) custom-call(bf16[256,128]{1,0:T(8,128)(2,1)} %bitcast.12, bf16[256,128]{1,0:T(8,128)(2,1)} %bitcast.13, bf16[3,384,128]{2,1,0:T(8,128)(2,1)} %bitcast.10, bf16[3,384,128]{2,1,0:T(8,128)(2,1)} %bitcast.11, s32[8,128]{1,0:T(8,128)} %bitcast.14, ...), custom_call_target="tpu_custom_call" | custom-call | tf_op jit(solution)/shard_map/pallas_call | solution.py:649
  45.5 2.1 %shard_map.166 = (bf16[256,128]{1,0:T(8,128)(2,1)}, bf16[256,128]{1,0:T(8,128)(2,1)}, f32[1152,128]{1,0:T(8,128)}, f32[1152,128]{1,0:T(8,128)}) custom-call(bf16[256,128]{1,0:T(8,128)(2,1)} %get-tuple-element.11.out_in, bf16[256,128]{1,0:T(8,128)(2,1)} %get-tuple-element.12.fgrad_in, bf16[2,16,80,128]{3,2,1,0:T(8,128)(2,1)} %get-tuple-element.13.sums_from), custom_call_target="tpu_custom_call" | custom-call | tf_op jit(solution)/shard_map/pallas_call | solution.py:697
